TPU v7x, 256 devices: a whole 4x4x8 slice. The times are simulated.
256 devices in a mesh: slab: 8 (over y, core), dom: 32 (over z, x).
Axes of the slice: x: 4, y: 4, z: 8, core: 2. Of those that a mesh axis runs over, the one named last changes fastest.
Arguments:
- reference_blocks: bfloat16 [55296, 2, 128], P('slab'), may hold values from -6 to 6
- corner_maps: bfloat16 [8, 128, 128], replicated, may hold values from -0.1875 to 0.1875
- volumes: bfloat16 [256, 32, 32, 32], P(('slab', 'dom')), may hold values from -6 to 6
- wedge: int32 [256, 32768], P(('slab', 'dom')), may hold values 0 or 1
- source_slab: int32 [256, 8, 256, 1], P(('slab', 'dom')), may hold values from 0 to 7; in each aligned block of 256 rows (0 to 255, 256 to 511, ..., all dimensions but the last counted through in order) at most 64 rows name the same one
- block_offset: int32 [256, 8, 256], P(('slab', 'dom')), may hold values from 0 to 6911
- flags: int32 [256], P(('slab', 'dom')), may hold values 0 or 1
- shifts: float32 [256, 24], P(('slab', 'dom')), may hold values from -2 to 2
- past_steps: float32 [4, 256, 24], P(None, ('slab', 'dom')), may hold values from -12 to 12
- past_changes: float32 [4, 256, 24], P(None, ('slab', 'dom')), may hold values from -30 to 30
Outputs:
- scores: float32 [256, 8], P(('slab', 'dom'))
- new_shifts: float32 [256, 24], P(('slab', 'dom'))
Inputs may be any that keep to these rules, and one draw needn't show every extreme that they name: `source_slab`: in the 256 blocks of one particle's trial at most 64 name one slab, and some trials name one slab exactly 64 times.
All inputs are finite; a program needn't handle non-finite values. No bound on the sum of `wedge` or of `flags` on one device may be relied on, other than what follows from the above.
Results may differ from a plain program's by a relative error of at most 0.0028.
Values may be sent and summed in bfloat16 or wider, within the bound.
A program may use at most 128 MiB of HBM per device.

v0:
```python
import math

import jax
import jax.numpy as jnp
from jax import lax
from jax.sharding import PartitionSpec as P

CORNERS = 8
HIST = 4


def signed_frequency(edge_len):
    index_line = jnp.arange(edge_len, dtype=jnp.int32)
    return jnp.where(index_line < edge_len // 2, index_line, index_line - edge_len).astype(
        jnp.float32
    )


def frequency_grid(edge_len):
    freq_line = signed_frequency(edge_len)
    full_shape = (edge_len, edge_len, edge_len)
    freq_one = jnp.broadcast_to(freq_line[:, None, None], full_shape).reshape(-1)
    freq_two = jnp.broadcast_to(freq_line[None, :, None], full_shape).reshape(-1)
    freq_three = jnp.broadcast_to(freq_line[None, None, :], full_shape).reshape(-1)
    return (freq_one, freq_two, freq_three)


def pose_terms(
    spectrum_real,
    spectrum_imag,
    box_real,
    box_imag,
    wedge_weight,
    shift_trio,
    freq_one,
    freq_two,
    freq_three,
    edge_len,
):
    cross_real = spectrum_real * box_real + spectrum_imag * box_imag
    cross_imag = spectrum_real * box_imag - spectrum_imag * box_real
    phase_step = 2.0 * math.pi / edge_len
    phases = phase_step * (
        freq_one * shift_trio[..., 0:1]
        + freq_two * shift_trio[..., 1:2]
        + freq_three * shift_trio[..., 2:3]
    )
    cosines = jnp.cos(phases)
    sines = jnp.sin(phases)
    power_particle = jnp.sum(
        wedge_weight * (spectrum_real * spectrum_real + spectrum_imag * spectrum_imag), axis=-1
    )
    power_box = jnp.sum(wedge_weight * (box_real * box_real + box_imag * box_imag), axis=-1)
    factor = math.sqrt(edge_len**3) / jnp.sqrt((power_particle + 1e-06) * (power_box + 1e-06))
    scores = factor * jnp.sum(wedge_weight * (cross_real * cosines + cross_imag * sines), axis=-1)
    rotation_part = wedge_weight * (cross_imag * cosines - cross_real * sines)
    slopes = jnp.stack(
        [
            jnp.sum(rotation_part * freq_one, axis=-1),
            jnp.sum(rotation_part * freq_two, axis=-1),
            jnp.sum(rotation_part * freq_three, axis=-1),
        ],
        axis=-1,
    )
    return (scores, factor[..., None] * phase_step * slopes)


def fourier_volume(volume):
    edge_len = volume.shape[1]
    highest = lax.Precision.HIGHEST
    index_line = jnp.arange(edge_len, dtype=jnp.int32)
    angles = (
        2.0
        * math.pi
        / edge_len
        * (index_line[:, None] * index_line[None, :] % edge_len).astype(jnp.float32)
    )
    cosine_table = jnp.cos(angles)
    sine_table = jnp.sin(angles)
    real_part = jnp.einsum("ux,pxyz->puyz", cosine_table, volume, precision=highest)
    imag_part = -jnp.einsum("ux,pxyz->puyz", sine_table, volume, precision=highest)
    next_real = jnp.einsum(
        "vy,puyz->puvz", cosine_table, real_part, precision=highest
    ) + jnp.einsum("vy,puyz->puvz", sine_table, imag_part, precision=highest)
    next_imag = jnp.einsum(
        "vy,puyz->puvz", cosine_table, imag_part, precision=highest
    ) - jnp.einsum("vy,puyz->puvz", sine_table, real_part, precision=highest)
    last_real = jnp.einsum(
        "wz,puvz->puvw", cosine_table, next_real, precision=highest
    ) + jnp.einsum("wz,puvz->puvw", sine_table, next_imag, precision=highest)
    last_imag = jnp.einsum(
        "wz,puvz->puvw", cosine_table, next_imag, precision=highest
    ) - jnp.einsum("wz,puvz->puvw", sine_table, next_real, precision=highest)
    return (last_real.reshape(volume.shape[0], -1), last_imag.reshape(volume.shape[0], -1))


def local(
    reference_blocks,
    corner_maps,
    volumes,
    wedge,
    source_slab,
    block_offset,
    flags,
    shifts,
    past_steps,
    past_changes,
):
    local_parts, trials, blocks = block_offset.shape
    slab_len = reference_blocks.shape[0]
    own_slab = source_slab[..., 0]
    row_lists = [
        own_slab * slab_len + (block_offset + corner) % slab_len for corner in range(CORNERS)
    ]
    wanted_rows = jnp.stack(row_lists).reshape(CORNERS, -1)
    shard_piece = lax.all_gather(reference_blocks, "slab", axis=0, tiled=True)
    piece_rows = shard_piece.shape[0]
    inside = (wanted_rows >= 0) & (wanted_rows < piece_rows)
    taken = jnp.take(shard_piece, jnp.clip(wanted_rows, 0, piece_rows - 1), axis=0)
    picked_all = jnp.where(inside[..., None, None], taken, jnp.zeros_like(taken))
    summed = jnp.zeros((wanted_rows.shape[1] * 2, 128), jnp.float32)
    for corner in range(CORNERS):
        summed = summed + jnp.dot(
            picked_all[corner].reshape(-1, 128),
            corner_maps[corner],
            preferred_element_type=jnp.float32,
        )
    boxes = summed.astype(jnp.bfloat16).reshape(local_parts, trials, blocks, 2, 128)
    edge_len = volumes.shape[1]
    freq_one, freq_two, freq_three = frequency_grid(edge_len)
    spectrum_real, spectrum_imag = fourier_volume(volumes.astype(jnp.float32))
    box_values = boxes.astype(jnp.float32)
    box_real = box_values[:, :, :, 0, :].reshape(local_parts, trials, -1)
    box_imag = box_values[:, :, :, 1, :].reshape(local_parts, trials, -1)
    wedge_weight = wedge.astype(jnp.float32)[:, None, :]
    scores, slopes = pose_terms(
        spectrum_real[:, None, :],
        spectrum_imag[:, None, :],
        box_real,
        box_imag,
        wedge_weight,
        shifts.reshape(local_parts, trials, 3),
        freq_one,
        freq_two,
        freq_three,
        edge_len,
    )
    active = (1 - flags).astype(jnp.float32)[:, None]
    gradient = -active * slopes.reshape(local_parts, -1)
    pair_dots, change_square = lax.psum(
        (
            jnp.sum(past_steps * past_changes, axis=(1, 2)),
            jnp.sum(past_changes[HIST - 1] * past_changes[HIST - 1]),
        ),
        ("slab", "dom"),
    )
    alpha_list = [None] * HIST
    direction = gradient
    for pair in reversed(range(HIST)):
        alpha_list[pair] = (
            lax.psum(jnp.sum(past_steps[pair] * direction), ("slab", "dom")) / pair_dots[pair]
        )
        direction = direction - alpha_list[pair] * past_changes[pair]
    result_dir = pair_dots[HIST - 1] / change_square * direction
    for pair in range(HIST):
        beta_now = (
            lax.psum(jnp.sum(past_changes[pair] * result_dir), ("slab", "dom")) / pair_dots[pair]
        )
        result_dir = result_dir + (alpha_list[pair] - beta_now) * past_steps[pair]
    new_shifts = shifts - active * result_dir
    return (scores, new_shifts)


def solution(mesh):
    return jax.shard_map(
        local,
        mesh=mesh,
        in_specs=(
            P("slab", None, None),
            P(),
            P(("slab", "dom"), None, None, None),
            P(("slab", "dom"), None),
            P(("slab", "dom"), None, None, None),
            P(("slab", "dom"), None, None),
            P(("slab", "dom")),
            P(("slab", "dom"), None),
            P(None, ("slab", "dom"), None),
            P(None, ("slab", "dom"), None),
        ),
        out_specs=(P(("slab", "dom"), None), P(("slab", "dom"), None)),
        check_vma=False,
    )
```

profile of v0, /device:TPU:1, one launch (start us, length us, event | category | flops | bytes accessed | tf_op | source)
XLA Modules:
  0.0 941.8 jit_solution(14144884351491195205)
XLA Ops:
  7.2 0.7 all-gather.2.cloned.1.call-update
  8.3 0.4 fusion.6
  8.8 0.3 copy.61
  9.1 0.5 convolution_negate_fusion
  9.9 0.6 fusion.39
  10.5 0.6 fusion.35
  11.2 0.6 fusion.2
  11.8 1.0 fusion.37
  12.8 0.6 fusion.1
  13.5 1.0 convolution_add_fusion.7
  14.6 1.0 fusion.33
  15.6 1.0 multiply_add_fusion.1
  17.7 0.5 broadcast.954
  18.2 0.7 reduce.21
  20.0 0.9 multiply_reduce_fusion.5
  22.2 128.1 %all-gather.2.cloned.1.call-done = bf16[55296,2,128]{2,1,0:T(2,128)(2,1)} async-done(((bf16[6912,2,128]{2,1,0:T(2,128)(2,1)}), bf16[55296,2,128]{2,1,0:T(2,128)(2,1)}) %all-gather.2.cloned.1.call-update) | async-done | bytes 28311568 | tf_op jit(solution)/shard_map/all_gather | solution.py:116
  150.3 114.8 %gather_fusion = bf16[16384,2,128]{2,1,0:T(2,128)(2,1)} fusion(bf16[55296,2,128]{2,1,0:T(2,128)(2,1)} %all-gather.2.cloned.1.call-done, s32[16384]{0:T(1024)S(1)} %broadcast_clamp_fusion), kind=kCustom, calls=%fused_computation | custom fusion | bytes 16842752 | tf_op jit(solution)/shard_map/jit(_take)/gather | solution.py:119
  265.1 41.5 %broadcast_select_fusion.1 = bf16[8,2048,2,128]{3,2,1,0:T(2,128)(2,1)S(1)} fusion(pred[8,2048]{1,0:T(8,128)(4,1)S(1)} %get-tuple-element.38, bf16[8,2048,2,128]{3,2,1,0:T(2,128)(2,1)} %bitcast.215, pred[8,2048]{1,0:T(8,128)(4,1)S(1)} %get-tuple-element.37), kind=kLoop, calls=%fused_computation.2 | loop fusion | flops 8388608 | bytes 16809984 | tf_op jit(solution)/shard_map/jit(_where)/select_n | solution.py:120
  306.6 5.9 fusion.130
  312.5 0.4 fusion.15
  312.9 0.4 convolution_add_fusion.6
  313.4 0.4 convolution_add_fusion.5
  313.8 0.4 convolution_add_fusion.4
  314.2 0.4 convolution_add_fusion.3
  314.6 0.4 convolution_add_fusion.2
  315.0 0.4 convolution_add_fusion.1
  315.5 0.4 fusion
  315.9 1.9 fusion.131
  317.8 5.1 multiply_reduce_fusion.4
  323.2 0.5 broadcast_multiply_fusion
  323.8 0.6 fusion.79
  324.5 76.7 %all-reduce.1 = (f32[]{:T(128)}, f32[4]{0:T(128)S(1)}) all-reduce(f32[]{:T(128)} %fusion.79, f32[4]{0:T(128)S(1)} %multiply_reduce_fusion.6), channel_id=1, replica_groups=mesh['slab'=8,'dom'=32] {'slab','dom'}, use_global_device_ids=true, to_apply=%region_11.12 | all-reduce | flops 5 | bytes 40 | tf_op jit(solution)/shard_map/psum | solution.py:161
  401.1 0.7 fusion.132
  403.1 0.6 fusion.77
  403.7 73.5 %psum.73 = f32[]{:T(128)} all-reduce(f32[]{:T(128)} %get-tuple-element.25), channel_id=1, replica_groups=mesh['slab'=8,'dom'=32] {'slab','dom'}, use_global_device_ids=true, to_apply=%region_13.14 | all-reduce | flops 1 | bytes 8 | tf_op jit(solution)/shard_map/psum | solution.py:161
  478.6 0.6 fusion.83
  479.2 73.3 %psum.74 = f32[]{:T(128)} all-reduce(f32[]{:T(128)} %get-tuple-element.14), channel_id=1, replica_groups=mesh['slab'=8,'dom'=32] {'slab','dom'}, use_global_device_ids=true, to_apply=%region_15.16 | all-reduce | flops 1 | bytes 8 | tf_op jit(solution)/shard_map/psum | solution.py:161
  553.8 0.6 fusion.69
  554.4 74.5 %all-reduce = (f32[]{:T(128)}, f32[]{:T(128)}) all-reduce(f32[]{:T(128)} %get-tuple-element.23, f32[]{:T(128)} %get-tuple-element.13), channel_id=1, replica_groups=mesh['slab'=8,'dom'=32] {'slab','dom'}, use_global_device_ids=true, to_apply=%region_17.18 | all-reduce | flops 2 | bytes 16 | tf_op jit(solution)/shard_map/psum | solution.py:161
  631.6 0.6 fusion.68
  632.2 73.4 %psum.76 = f32[]{:T(128)} all-reduce(f32[]{:T(128)} %get-tuple-element.21), channel_id=1, replica_groups=mesh['slab'=8,'dom'=32] {'slab','dom'}, use_global_device_ids=true, to_apply=%region_19.20 | all-reduce | flops 1 | bytes 8 | tf_op jit(solution)/shard_map/psum | solution.py:167
  707.0 0.6 fusion.72
  707.6 74.1 %psum.77 = f32[]{:T(128)} all-reduce(f32[]{:T(128)} %fusion.72), channel_id=1, replica_groups=mesh['slab'=8,'dom'=32] {'slab','dom'}, use_global_device_ids=true, to_apply=%region_21.22 | all-reduce | flops 1 | bytes 8 | tf_op jit(solution)/shard_map/psum | solution.py:167
  783.0 0.6 fusion.76
  783.6 73.4 %psum.78 = f32[]{:T(128)} all-reduce(f32[]{:T(128)} %get-tuple-element.19), channel_id=1, replica_groups=mesh['slab'=8,'dom'=32] {'slab','dom'}, use_global_device_ids=true, to_apply=%region_23.24 | all-reduce | flops 1 | bytes 8 | tf_op jit(solution)/shard_map/psum | solution.py:167
  858.3 0.6 fusion.85
  858.9 74.2 %psum.79 = f32[]{:T(128)} all-reduce(f32[]{:T(128)} %fusion.85), channel_id=1, replica_groups=mesh['slab'=8,'dom'=32] {'slab','dom'}, use_global_device_ids=true, to_apply=%region_25.26 | all-reduce | flops 1 | bytes 8 | tf_op jit(solution)/shard_map/psum | solution.py:167
  934.4 0.5 fusion.82
  (68 shorter events, 3.2 us)
Async XLA Ops:
  7.2 1.1 copy-start
  7.2 0.8 copy-start.7
  7.2 0.8 copy-start.6
  7.2 143.1 %all-gather.2.cloned.1.call-start = ((), (), s32[]{:S(2)}) async-start(), calls=%async_computation | async-start | bytes 31850496 | tf_op jit(solution)/shard_map/all_gather | solution.py:116
  16.7 1.6 copy-start.8
  16.7 2.3 copy-start.2
  17.0 4.8 copy-start.4
  17.0 4.8 copy-start.5
  306.6 5.9 copy-start.3
  315.9 619.1 %copy-start.1 = (bf16[1,32,32,32]{3,2,1,0:T(8,128)(2,1)S(1)}, bf16[1,32,32,32]{3,2,1,0:T(8,128)(2,1)}, u32[]{:S(2)}) copy-start(bf16[1,32,32,32]{3,2,1,0:T(8,128)(2,1)} %param.12) | copy-start | bytes 196612
Sparse Core Ops, SparseCore 0:
  9.9 140.4 all-gather.1
where the time goes:
time: 944 us; the launch traced here: 942 us
  blocking collectives  593 us (63%)
  waiting for transfers between devices  129 us (14%)
  local copies, waits for them, and re-layouts  127 us (13%)
  other arithmetic  54.6 us (6%)
  between operations  27.7 us (3%)
  matrix products  10.8 us (1%)
    psum x4, blocking collectives, local(): lax.psum(jnp.sum(past_steps[pair] * direction), ('slab', 'dom'))  298 us
    psum x4, blocking collectives, local(): lax.psum(jnp.sum(past_changes[pair] * result_dir), ('slab', 'dom'))  295 us
    all_gather x1, waiting for transfers between devices, local(): shard_piece = lax.all_gather(reference_blocks, 'slab', axis=0, tiled=True)  128 us
    gather x1, local copies, waits for them, and re-layouts, local(): jnp.take(shard_piece, jnp.clip(wanted_rows, 0, piece_rows - 1), axis=0)  115 us
    select_n x1, other arithmetic, local(): jnp.where(inside[..., None, None], taken, jnp.zeros_like(taken))  41.5 us
  transfers between devices with their start and end apart: 1, of which 1 were waited for; matrix products, arithmetic and copies ran while one was open for 1% of the time, Pallas kernels for 0%

commit v1 on v0

--- a/solution.py
+++ b/solution.py
@@ -7,6 +7,7 @@
 
 CORNERS = 8
 HIST = 4
+CAP = 64
 
 
 def signed_frequency(edge_len):
@@ -108,24 +109,35 @@
 ):
     local_parts, trials, blocks = block_offset.shape
     slab_len = reference_blocks.shape[0]
-    own_slab = source_slab[..., 0]
-    row_lists = [
-        own_slab * slab_len + (block_offset + corner) % slab_len for corner in range(CORNERS)
-    ]
-    wanted_rows = jnp.stack(row_lists).reshape(CORNERS, -1)
-    shard_piece = lax.all_gather(reference_blocks, "slab", axis=0, tiled=True)
-    piece_rows = shard_piece.shape[0]
-    inside = (wanted_rows >= 0) & (wanted_rows < piece_rows)
-    taken = jnp.take(shard_piece, jnp.clip(wanted_rows, 0, piece_rows - 1), axis=0)
-    picked_all = jnp.where(inside[..., None, None], taken, jnp.zeros_like(taken))
-    summed = jnp.zeros((wanted_rows.shape[1] * 2, 128), jnp.float32)
+    slabs = lax.axis_size("slab")
+    own_slab = source_slab[0, :, :, 0]
+    offsets = block_offset[0]
+    extended = jnp.concatenate([reference_blocks, reference_blocks[: CORNERS - 1]], axis=0)
+    summed = jnp.zeros((slab_len * 2, 128), jnp.float32)
     for corner in range(CORNERS):
         summed = summed + jnp.dot(
-            picked_all[corner].reshape(-1, 128),
+            extended[corner : corner + slab_len].reshape(-1, 128),
             corner_maps[corner],
             preferred_element_type=jnp.float32,
         )
-    boxes = summed.astype(jnp.bfloat16).reshape(local_parts, trials, blocks, 2, 128)
+    mapped = summed.astype(jnp.bfloat16).reshape(slab_len, 256)
+    named = (own_slab[:, :, None] == jnp.arange(slabs)[None, None, :]).astype(jnp.int32)
+    ranks = jnp.sum((jnp.cumsum(named, axis=1) - named) * named, axis=2)
+    slot_of = own_slab * CAP + ranks
+    placed = slot_of[:, :, None] == jnp.arange(slabs * CAP)[None, None, :]
+    asked = jnp.sum(jnp.where(placed, offsets[:, :, None], 0), axis=1)
+    asked = asked.reshape(trials, slabs, CAP).transpose(1, 0, 2)
+    wanted = lax.all_to_all(asked, "slab", 0, 0, tiled=True)
+    picked = jnp.take(mapped, wanted.reshape(-1), axis=0, mode="clip")
+    landed = lax.all_to_all(picked.reshape(slabs, trials * CAP, 256), "slab", 0, 0, tiled=True)
+    landed = landed.reshape(slabs, trials, CAP, 256).transpose(1, 0, 2, 3)
+    boxes = jnp.einsum(
+        "tbk,tkj->tbj",
+        placed.astype(jnp.bfloat16),
+        landed.reshape(trials, slabs * CAP, 256),
+        preferred_element_type=jnp.float32,
+    )
+    boxes = boxes.reshape(1, trials, blocks, 2, 128)
     edge_len = volumes.shape[1]
     freq_one, freq_two, freq_three = frequency_grid(edge_len)
     spectrum_real, spectrum_imag = fourier_volume(volumes.astype(jnp.float32))
@@ -147,26 +159,19 @@
     )
     active = (1 - flags).astype(jnp.float32)[:, None]
     gradient = -active * slopes.reshape(local_parts, -1)
-    pair_dots, change_square = lax.psum(
-        (
-            jnp.sum(past_steps * past_changes, axis=(1, 2)),
-            jnp.sum(past_changes[HIST - 1] * past_changes[HIST - 1]),
-        ),
-        ("slab", "dom"),
-    )
+    basis = jnp.concatenate([past_steps[:, 0], past_changes[:, 0], gradient], axis=0)
+    gram = lax.psum(jnp.sum(basis[:, None, :] * basis[None, :, :], axis=-1), ("slab", "dom"))
+    pair_dots = [gram[pair, HIST + pair] for pair in range(HIST)]
+    held = jnp.zeros((2 * HIST + 1,), jnp.float32).at[2 * HIST].set(1.0)
     alpha_list = [None] * HIST
-    direction = gradient
     for pair in reversed(range(HIST)):
-        alpha_list[pair] = (
-            lax.psum(jnp.sum(past_steps[pair] * direction), ("slab", "dom")) / pair_dots[pair]
-        )
-        direction = direction - alpha_list[pair] * past_changes[pair]
-    result_dir = pair_dots[HIST - 1] / change_square * direction
+        alpha_list[pair] = jnp.sum(gram[pair] * held) / pair_dots[pair]
+        held = held.at[HIST + pair].add(-alpha_list[pair])
+    held = pair_dots[HIST - 1] / gram[2 * HIST - 1, 2 * HIST - 1] * held
     for pair in range(HIST):
-        beta_now = (
-            lax.psum(jnp.sum(past_changes[pair] * result_dir), ("slab", "dom")) / pair_dots[pair]
-        )
-        result_dir = result_dir + (alpha_list[pair] - beta_now) * past_steps[pair]
+        beta_now = jnp.sum(gram[HIST + pair] * held) / pair_dots[pair]
+        held = held.at[pair].add(alpha_list[pair] - beta_now)
+    result_dir = jnp.sum(held[:, None] * basis, axis=0)[None]
     new_shifts = shifts - active * result_dir
     return (scores, new_shifts)
 

time: 944 us -> 340 us (0.36)
  blocking collectives: 593 us -> 78.3 us
  waiting for transfers between devices: 129 us -> 2.11 us
  other arithmetic: 54.6 us -> 160 us
  local copies, waits for them, and re-layouts: 127 us -> 45.3 us
  matrix products: 10.8 us -> 27.3 us
  between operations: 27.7 us -> 14.2 us
  starting transfers between devices: 0.04 us -> 11.4 us
    psum x8 -> x1, blocking collectives: 593 us -> 78.3 us  [local(): lax.psum(jnp.sum(basis[:, None, :] * basis[None, :, :], axis=-1), ('slab'...]
    concatenate x0 -> x3, other arithmetic: none -> 135 us  [the longest x2 135 us: local(): jnp.concatenate([reference_blocks, reference_blocks[:CORNERS - 1]], axis=0)]
    all_gather x1 -> x0, waiting for transfers between devices: 128 us -> none  [local(): shard_piece = lax.all_gather(reference_blocks, 'slab', axis=0, tiled=True)]
    gather x1, local copies, waits for them, and re-layouts: 115 us -> 18.2 us  [local(): picked = jnp.take(mapped, wanted.reshape(-1), axis=0, mode='clip')]
    select_n x2 -> x0, other arithmetic: 41.6 us -> none  [the longest x1 41.5 us: local(): jnp.where(inside[..., None, None], taken, jnp.zeros_like(taken))]
    all_to_all x0 -> x2, starting transfers between devices: none -> 11.4 us  [the longest x1 6.48 us: local(): wanted = lax.all_to_all(asked, 'slab', 0, 0, tiled=True)]
    dot_general x8 -> x9, matrix products: 3.34 us -> 14.1 us  [the longest x8 12.5 us: local(): jnp.dot(extended[corner:corner + slab_len].reshape(-1, 128), corner_maps[...]
  transfers between devices with their start and end apart: 1 -> 2, of which waited for: 1 -> 1; matrix products, arithmetic and copies ran while one was open for 1% -> 53% of each run, Pallas kernels for 0% -> 0%
where the time goes in v1:
time: 340 us; the launch traced here: 338 us
  other arithmetic  160 us (47%)
  blocking collectives  78.3 us (23%)
  local copies, waits for them, and re-layouts  45.3 us (13%)
  matrix products  27.3 us (8%)
  between operations  14.2 us (4%)
  starting transfers between devices  11.4 us (3%)
    concatenate x2, other arithmetic, local(): jnp.concatenate([reference_blocks, reference_blocks[:CORNERS - 1]], axis=0)  135 us
    psum x1, blocking collectives, local(): lax.psum(jnp.sum(basis[:, None, :] * basis[None, :, :], axis=-1), ('slab'...  78.3 us
    gather x1, local copies, waits for them, and re-layouts, local(): picked = jnp.take(mapped, wanted.reshape(-1), axis=0, mode='clip')  18.2 us
    dot_general x8, matrix products, local(): jnp.dot(extended[corner:corner + slab_len].reshape(-1, 128), corner_maps[...  12.5 us
    unnamed x54, local copies, waits for them, and re-layouts  9.46 us
  transfers between devices with their start and end apart: 2, of which 1 were waited for; matrix products, arithmetic and copies ran while one was open for 53% of the time, Pallas kernels for 0%

profile of v1, /device:TPU:1, one launch (start us, length us, event | category | flops | bytes accessed | tf_op | source)
XLA Modules:
  0.0 338.3 jit_solution(5482432112638379032)
XLA Ops:
  0.6 0.7 copy.128
  1.4 0.7 fusion.18
  2.1 4.5 %reduce-window.6 = s32[8,8,2,128]{3,1,2,0:T(8,128)S(1)} reduce-window(s32[8,8,2,128]{3,1,2,0:T(8,128)S(1)} %fusion.18, s32[]{:T(128)} %constant.237.clone.1), window={size=1x1x1x128 pad=0_0x0_0x0_0x127_0}, to_apply=%region_1.2 | reduce-window | flops 2080768 | bytes 131076 | tf_op jit(solution)/shard_map/reduce-window
  7.0 0.7 multiply_add_fusion.2
  8.3 1.4 select_reduce_fusion
  10.5 6.5 %all-to-all-start = ((s32[8,1,512]{2,1,0:T(1,128)}), s32[8,1,512]{2,1,0:T(1,128)S(1)}, u32[]{:S(2)}, u32[]{:S(2)}) async-start(s32[8,1,512]{2,1,0:T(1,128)} %reshape.1183), calls=%async_computation | async-start | bytes 32768 | tf_op jit(solution)/shard_map/all_to_all | solution.py:130
  17.0 0.7 slice.213
  17.7 113.4 %pad_maximum_fusion = (bf16[6912,2,128]{2,1,0:T(2,128)(2,1)}, bf16[6912,2,128]{2,1,0:T(2,128)(2,1)}, bf16[6912,2,128]{2,1,0:T(2,128)(2,1)}, bf16[6912,2,128]{2,1...) fusion(bf16[7,2,128]{2,1,0:T(2,128)(2,1)S(1)} %slice.213, bf16[6912,2,128]{2,1,0:T(2,128)(2,1)} %param.28), kind=kLoop, calls=%fused_computation.24 | loop fusion | flops 10616832 | bytes 24776192 | tf_op jit(solution)/shard_map/concatenate | solution.py:115
  131.2 21.2 %fusion.2 = bf16[6912,2,128]{2,1,0:T(2,128)(2,1)} fusion(bf16[7,2,128]{2,1,0:T(2,128)(2,1)S(1)} %slice.213, bf16[6912,2,128]{2,1,0:T(2,128)(2,1)S(1)} %copy-done.2), kind=kLoop, calls=%fused_computation.18 | loop fusion | flops 1769472 | bytes 7081472 | tf_op jit(solution)/shard_map/concatenate | solution.py:115
  154.6 3.3 fusion.26
  157.9 1.1 convolution_add_fusion.6
  159.0 0.9 copy-done.8
  159.9 1.1 convolution_add_fusion.5
  160.9 0.9 copy-done.7
  161.9 1.1 convolution_add_fusion.4
  162.9 0.9 copy-done.6
  163.9 1.1 convolution_add_fusion.3
  165.0 0.9 copy-done.5
  165.9 1.1 convolution_add_fusion.2
  166.9 0.9 copy-done.4
  167.9 1.1 convolution_add_fusion.1
  169.0 0.9 copy-done.3
  169.9 2.8 fusion
  172.7 1.4 fusion.10
  174.1 4.8 %reshape.1145 = bf16[6912,256]{1,0:T(8,128)(2,1)S(1)} reshape(bf16[13824,128]{1,0:T(8,128)(2,1)} %fusion) | data formatting | bytes 7077888 | tf_op jit(solution)/shard_map/reshape | solution.py:123
  180.1 1.4 reduce.41
  182.2 0.8 reshape.1162
  183.6 18.2 %gather_fusion = bf16[4096,256]{1,0:T(8,128)(2,1)} fusion(bf16[6912,256]{1,0:T(8,128)(2,1)S(1)} %reshape.1145, s32[4096]{0:T(1024)} %broadcast_clamp_fusion), kind=kCustom, calls=%fused_computation | custom fusion | bytes 4210688 | tf_op jit(solution)/shard_map/jit(_take)/gather | solution.py:131
  201.9 4.9 %all-to-all-start.1 = ((bf16[8,512,256]{2,1,0:T(8,128)(2,1)}), bf16[8,512,256]{2,1,0:T(8,128)(2,1)S(1)}, u32[]{:S(2)}, u32[]{:S(2)}) async-start(bf16[8,512,256]{2,1,0:T(8,128)(2,1)} %bitcast.191), calls=%async_computation.1 | async-start | bytes 4194304 | tf_op jit(solution)/shard_map/all_to_all | solution.py:132
  206.8 1.7 fusion.46
  208.5 1.0 fusion.48
  209.5 1.4 fusion.9
  210.9 2.0 convolution_add_fusion.7
  213.2 2.0 fusion.44
  215.2 2.0 multiply_add_fusion.1
  217.2 1.3 mul.625
  218.8 0.8 mul.628
  219.6 1.0 copy.111
  220.8 0.8 mul.633
  221.6 1.6 copy.112
  223.3 0.8 mul.638
  224.1 1.0 copy.113
  226.4 1.0 convert_element_type.64
  228.4 1.8 multiply_reduce_fusion.5
  231.0 2.1 all-to-all-done.1
  233.3 1.6 fusion.1
  235.0 5.2 %multiply_reduce_fusion.4 = (f32[8]{0:T(128)S(1)}, f32[8]{0:T(128)S(1)}, f32[8]{0:T(128)S(1)}, f32[8]{0:T(128)S(1)}, f32[8]{0:T(128)S(1)}) fusion(f32[1,8,256,2,128]{2,4,3,1,0:T(8,128)S(1)} %bitcast.192, f32[256,128]{0,1:T(8,128)S(1)} %copy.103, f32[8]{0:T(128)S(1)} %get-tuple-element.119, f32[256,128]{0,1:T(8,128)S(1)} %copy.113, ...), kind=kLoop, calls=%fused_computation.43 | loop fusion | flops 8388568 | bytes 2883840 | tf_op jit(solution)/shard_map/reduce_sum | solution.py:54
  241.2 78.3 %psum.7 = f32[9,9]{1,0:T(8,128)S(1)} all-reduce(f32[9,9]{1,0:T(8,128)S(1)} %multiply_reduce_fusion.6), channel_id=1, replica_groups=mesh['slab'=8,'dom'=32] {'slab','dom'}, use_global_device_ids=true, to_apply=%region_11.12 | all-reduce | flops 81 | bytes 648 | tf_op jit(solution)/shard_map/psum | solution.py:163
  (104 shorter events, 17.0 us)
Async XLA Ops:
  0.6 151.7 %copy-start = (bf16[1,32,32,32]{3,2,1,0:T(8,128)(2,1)S(1)}, bf16[1,32,32,32]{3,2,1,0:T(8,128)(2,1)}, u32[]{:S(2)}) copy-start(bf16[1,32,32,32]{3,2,1,0:T(8,128)(2,1)} %param.30) | copy-start | bytes 196612
  7.7 0.6 copy-start.18
  10.5 168.5 %all-to-all-start = ((s32[8,1,512]{2,1,0:T(1,128)}), s32[8,1,512]{2,1,0:T(1,128)S(1)}, u32[]{:S(2)}, u32[]{:S(2)}) async-start(s32[8,1,512]{2,1,0:T(1,128)} %reshape.1183), calls=%async_computation | async-start | bytes 32768 | tf_op jit(solution)/shard_map/all_to_all | solution.py:130
  17.7 113.4 %copy-start.2 = (bf16[6912,2,128]{2,1,0:T(2,128)(2,1)S(1)}, bf16[6912,2,128]{2,1,0:T(2,128)(2,1)}, u32[]{:S(2)}) copy-start(bf16[6912,2,128]{2,1,0:T(2,128)(2,1)} %param.28) | copy-start | bytes 10616836
  152.3 2.2 copy-start.16
  153.5 4.3 %copy-start.11 = (f32[32,32,32]{1,2,0:T(8,128)}, f32[32,32,32]{1,2,0:T(8,128)S(1)}, u32[]{:S(2)}) copy-start(f32[32,32,32]{1,2,0:T(8,128)S(1)} %copy.94) | copy-start | bytes 393220
  154.5 18.2 %copy-start.13 = (f32[32,32,32]{1,2,0:T(8,128)}, f32[32,32,32]{1,2,0:T(8,128)S(1)}, u32[]{:S(2)}) copy-start(f32[32,32,32]{1,2,0:T(8,128)S(1)} %copy.96) | copy-start | bytes 393220
  154.5 3.3 copy-start.9
  157.9 2.0 copy-start.8
  159.9 2.0 copy-start.7
  161.9 2.0 copy-start.6
  163.9 2.0 copy-start.5
  165.9 2.0 copy-start.4
  167.9 2.0 copy-start.3
  179.0 0.6 copy-start.17
  201.8 6.6 %copy-start.10 = (f32[32,32,32]{1,2,0:T(8,128)S(1)}, f32[32,32,32]{1,2,0:T(8,128)}, u32[]{:S(2)}) copy-start(f32[32,32,32]{1,2,0:T(8,128)} %fusion.10) | copy-start | bytes 393220
  201.9 7.6 %copy-start.12 = (f32[32,32,32]{1,2,0:T(8,128)S(1)}, f32[32,32,32]{1,2,0:T(8,128)}, u32[]{:S(2)}) copy-start(f32[32,32,32]{1,2,0:T(8,128)} %copy-done.11) | copy-start | bytes 393220
  201.9 31.3 %all-to-all-start.1 = ((bf16[8,512,256]{2,1,0:T(8,128)(2,1)}), bf16[8,512,256]{2,1,0:T(8,128)(2,1)S(1)}, u32[]{:S(2)}, u32[]{:S(2)}) async-start(bf16[8,512,256]{2,1,0:T(8,128)(2,1)} %bitcast.191), calls=%async_computation.1 | async-start | bytes 4194304 | tf_op jit(solution)/shard_map/all_to_all | solution.py:132
  215.2 10.4 %copy-start.23 = (f32[1,24]{1,0:T(1,128)S(1)}, f32[1,24]{1,0:T(1,128)}, u32[]{:S(2)}) copy-start(f32[1,24]{1,0:T(1,128)} %param.35) | copy-start | bytes 292
  217.2 10.3 %copy-start.14 = (f32[32,32,32]{2,1,0:T(8,128)S(1)}, f32[32,32,32]{2,1,0:T(8,128)}, u32[]{:S(2)}) copy-start(f32[32,32,32]{2,1,0:T(8,128)} %get-tuple-element.136) | copy-start | bytes 393220
  223.2 10.1 %copy-start.19 = (s32[8,256]{1,0:T(8,128)S(1)}, s32[8,256]{1,0:T(8,128)}, u32[]{:S(2)}) copy-start(s32[8,256]{1,0:T(8,128)} %copy-done.18) | copy-start | bytes 24580
  233.1 1.9 copy-start.15
  233.3 105.0 %copy-start.1 = (bf16[1,32,32,32]{3,2,1,0:T(8,128)(2,1)S(1)}, bf16[1,32,32,32]{3,2,1,0:T(8,128)(2,1)}, u32[]{:S(2)}) copy-start(bf16[1,32,32,32]{3,2,1,0:T(8,128)(2,1)} %param.30) | copy-start | bytes 196612
  233.3 7.8 %copy-start.20 = (f32[4,1,24]{2,1,0:T(1,128)S(1)}, f32[4,1,24]{2,1,0:T(1,128)}, u32[]{:S(2)}) copy-start(f32[4,1,24]{2,1,0:T(1,128)} %param.37) | copy-start | bytes 1156
  233.3 7.8 %copy-start.21 = (f32[4,1,24]{2,1,0:T(1,128)S(1)}, f32[4,1,24]{2,1,0:T(1,128)}, u32[]{:S(2)}) copy-start(f32[4,1,24]{2,1,0:T(1,128)} %param.36) | copy-start | bytes 1156
  233.3 86.8 %copy-start.24 = (f32[1,9]{1,0:T(1,128)S(1)}, f32[1,9]{1,0:T(1,128)}, u32[]{:S(2)}) copy-start(f32[1,9]{1,0:T(1,128)} %constant.248.clone.1) | copy-start | bytes 112
  233.3 90.1 %copy-start.22 = (f32[9]{0:T(128)S(1)}, f32[9]{0:T(128)}, u32[]{:S(2)}) copy-start(f32[9]{0:T(128)} %constant.247.clone.1) | copy-start | bytes 112

commit v2 on v0

v2 whole, which is shorter than its diff:
```python
import functools
import math

import jax
import jax.numpy as jnp
import numpy as np
from jax import lax
from jax.experimental import pallas as pl
from jax.experimental.pallas import tpu as pltpu
from jax.sharding import PartitionSpec as P

CORNERS = 8
HIST = 4
CAP = 64
EDGE = 32
TRIALS = 8
BLOCKS = 256
LANES = 128
SLABS = 8
MESH = pl.DeviceIdType.MESH
CHUNK = 768
F32 = jnp.float32
BF16 = jnp.bfloat16


def split_pair(table):
    high = table.astype(BF16)
    low = (table - high.astype(np.float64)).astype(BF16)
    return np.stack([high, low])


@functools.lru_cache(maxsize=None)
def transform_tables():
    lane = np.arange(LANES)
    row = np.arange(BLOCKS)
    turn = -2j * np.pi
    inner = np.exp(
        turn
        * (
            (lane // 32)[:, None] * (lane // 32)[None, :] / 4
            + (lane % 32)[:, None] * (lane % 32)[None, :] / 32
        )
    )
    twiddle = np.exp(turn * np.arange(8)[:, None] * (lane // 32)[None, :] / 32)
    outer = np.exp(
        turn
        * (
            (row // 8)[:, None] * (row // 8)[None, :] / 32
            + (row % 8)[:, None] * (row % 8)[None, :] / 8
        )
    )
    inner_pair = split_pair(np.concatenate([inner.real, inner.imag], axis=1))
    outer_pair = split_pair(np.concatenate([outer.real, outer.imag], axis=0))
    return inner_pair, outer_pair, np.stack([twiddle.real, twiddle.imag]).astype(np.float32)


def dot(left, right):
    return jnp.dot(left, right, preferred_element_type=F32)


def signed(index):
    return jnp.where(index < EDGE // 2, index, index - EDGE).astype(F32)


def step_kernel(
    rows_ref,
    maps_ref,
    volume_ref,
    wedge_ref,
    slab_ref,
    offset_ref,
    flag_ref,
    shift_smem,
    shift_ref,
    steps_ref,
    changes_ref,
    inner_ref,
    outer_ref,
    twiddle_ref,
    scores_ref,
    new_ref,
    mapped,
    asked_out,
    asked_in,
    asked_smem,
    staged,
    sent,
    landed,
    hot,
    weighted,
    phase_tables,
    line_tables,
    line_smem,
    partial,
    basis,
    sum_slab,
    sum_z,
    sum_x,
    sum_out,
    ask_send,
    ask_recv,
    ask_local,
    data_send,
    data_recv,
    line_local,
    sum_send,
    sum_recv,
):
    slab = lax.axis_index("slab")
    dom = lax.axis_index("dom")
    z_at, x_at = dom // 4, lax.rem(dom, 4)
    slab_peers = [(lax.rem(slab + d, 8), dom) for d in range(1, 8)]
    z_peers = [(slab, lax.rem(z_at + d, 8) * 4 + x_at) for d in range(1, 8)]
    x_peers = [(slab, z_at * 4 + lax.rem(x_at + d, 4)) for d in range(1, 4)]

    barrier = pltpu.get_barrier_semaphore()
    for peer in slab_peers + z_peers + x_peers:
        pl.semaphore_signal(barrier, inc=1, device_id=peer, device_id_type=MESH)

    slab_rows = [slab_ref[t] for t in range(TRIALS)]
    slab_iota = lax.broadcasted_iota(jnp.int32, (SLABS, BLOCKS), 0)
    named = jnp.concatenate(
        [jnp.where(slab_rows[t] == slab_iota, 1.0, 0.0) for t in range(TRIALS)], axis=0
    )
    below = lax.broadcasted_iota(jnp.int32, (BLOCKS, BLOCKS), 0)
    above = lax.broadcasted_iota(jnp.int32, (BLOCKS, BLOCKS), 1)
    before = jnp.where(below < above, 1.0, 0.0).astype(BF16)
    counts = dot(named.astype(BF16), before) * named
    slots = jnp.concatenate(
        [
            slab_rows[t].astype(F32) * CAP
            + jnp.sum(counts[t * SLABS : (t + 1) * SLABS], axis=0, keepdims=True)
            for t in range(TRIALS)
        ],
        axis=0,
    )
    offsets = offset_ref[...]
    high = offsets // LANES
    digits = jnp.concatenate([high, offsets - high * LANES], axis=0).astype(F32).astype(BF16)
    slot_iota = lax.broadcasted_iota(jnp.int32, (SLABS * CAP, BLOCKS), 0).astype(F32)
    trial_iota = lax.broadcasted_iota(jnp.int32, (TRIALS, SLABS * CAP), 0)
    asked = jnp.zeros((TRIALS, SLABS * CAP), F32)
    for t in range(TRIALS):
        placed = jnp.where(slot_iota == slots[t : t + 1], 1.0, 0.0).astype(BF16)
        found = lax.dot_general(
            digits, placed, (((1,), (1,)), ((), ())), preferred_element_type=F32
        )
        asked = jnp.where(
            trial_iota == t, found[:TRIALS] * LANES + found[TRIALS:], asked
        )
    asked = asked.astype(jnp.int32) * 2 + 8
    lane4 = lax.broadcasted_iota(jnp.int32, (4, LANES), 1)
    for s in range(SLABS):
        tile = asked[:, (s // 2) * LANES : (s // 2 + 1) * LANES]
        turned = pltpu.roll(tile, CAP, 1)
        if s % 2 == 0:
            both = jnp.where(lane4 < CAP, tile[:4], turned[4:])
        else:
            both = jnp.where(lane4 < CAP, turned[:4], tile[4:])
        asked_out[s] = jnp.concatenate([both, jnp.zeros((4, LANES), jnp.int32)], axis=0)

    pl.semaphore_wait(barrier, 17)

    def ask(peer):
        return pltpu.make_async_remote_copy(
            src_ref=asked_out.at[peer],
            dst_ref=asked_in.at[slab],
            send_sem=ask_send.at[peer],
            recv_sem=ask_recv.at[slab],
            device_id=(peer, dom),
            device_id_type=MESH,
        )

    for d in range(1, 8):
        ask(lax.rem(slab + d, 8)).start()
    asked_in[slab] = asked_out[slab]

    maps = jnp.concatenate(
        [maps_ref[:4].reshape(512, LANES), maps_ref[4:].reshape(512, LANES)], axis=1
    )
    row_count = rows_ref.shape[0]

    def map_chunk(base, rows):
        wide = jnp.concatenate([rows[2 * m : 2 * m + CHUNK] for m in range(4)], axis=1)
        both = dot(wide, maps)
        mapped[pl.ds(pl.multiple_of(base + 8, 8), CHUNK), :] = both[:, :LANES]
        mapped[pl.ds(pl.multiple_of(base, 8), CHUNK), :] += both[:, LANES:]

    mapped[0:8, :] = jnp.zeros((8, LANES), F32)

    def map_step(i, carry):
        base = pl.multiple_of(i * CHUNK, CHUNK)
        map_chunk(base, rows_ref[pl.ds(base, CHUNK + 16), :])
        return carry

    lax.fori_loop(0, row_count // CHUNK - 1, map_step, 0)
    map_chunk(
        row_count - CHUNK,
        jnp.concatenate([rows_ref[row_count - CHUNK :, :], rows_ref[:16, :]], axis=0),
    )
    mapped[row_count : row_count + 8, :] += mapped[0:8, :]

    for d in range(1, 8):
        peer = lax.rem(slab + d, 8)
        pltpu.make_async_remote_copy(
            src_ref=asked_out.at[peer],
            dst_ref=asked_in.at[peer],
            send_sem=ask_send.at[peer],
            recv_sem=ask_recv.at[peer],
            device_id=(peer, dom),
            device_id_type=MESH,
        ).wait_recv()
    to_smem = pltpu.make_async_copy(asked_in, asked_smem, ask_local)
    to_smem.start()
    to_smem.wait()

    def data(peer, u):
        return pltpu.make_async_remote_copy(
            src_ref=sent.at[peer, u],
            dst_ref=landed.at[slab, u],
            send_sem=data_send.at[peer, u],
            recv_sem=data_recv.at[slab, u],
            device_id=(peer, dom),
            device_id_type=MESH,
        )

    def pick(peer, u):
        for j in range(LANES):
            place = jnp.minimum(jnp.maximum(asked_smem[peer, u, j], 8), row_count + 6)
            staged[2 * j : 2 * j + 2, :] = mapped[pl.ds(place, 2), :]
        return staged[...].astype(BF16)

    def pick_trials(u, carry):
        def pick_peer(d, inner):
            peer = lax.rem(slab + d, 8)
            sent[peer, u] = pick(peer, u)
            data(peer, u).start()
            return inner

        lax.fori_loop(1, 8, pick_peer, 0)
        landed[slab, u] = pick(slab, u)
        return carry

    lax.fori_loop(0, 4, pick_trials, 0)

    volume = volume_ref[0].astype(F32)
    first = jnp.zeros((BLOCKS, 2 * LANES), F32)
    for g in range(4):
        part = volume[:, 8 * g : 8 * g + 8, :].reshape(BLOCKS, EDGE).astype(BF16)
        first = first + dot(part, inner_ref[0, 32 * g : 32 * g + 32, :])
        first = first + dot(part, inner_ref[1, 32 * g : 32 * g + 32, :])
    first = first.reshape(EDGE, 8, 2 * LANES)
    first_r, first_i = first[:, :, :LANES], first[:, :, LANES:]
    turn_r, turn_i = twiddle_ref[0][None], twiddle_ref[1][None]
    second = jnp.concatenate(
        [first_r * turn_r - first_i * turn_i, first_r * turn_i + first_i * turn_r], axis=-1
    ).reshape(BLOCKS, 2 * LANES)
    second_high = second.astype(BF16)
    second_low = (second - second_high.astype(F32)).astype(BF16)
    third = (
        dot(outer_ref[0], second_high)
        + dot(outer_ref[0], second_low)
        + dot(outer_ref[1], second_high)
    )
    spec_r = third[:BLOCKS, :LANES] - third[BLOCKS:, LANES:]
    spec_i = third[:BLOCKS, LANES:] + third[BLOCKS:, :LANES]
    weight = wedge_ref[...].astype(F32)
    weighted[0] = weight * spec_r
    weighted[1] = weight * spec_i
    weighted[2] = weight
    power_particle = jnp.sum(
        jnp.sum(weight * (spec_r * spec_r + spec_i * spec_i), axis=0, keepdims=True),
        axis=1,
        keepdims=True,
    )

    unit = 2.0 * math.pi / EDGE
    sub = lax.broadcasted_iota(jnp.int32, (8, LANES), 0)
    lane = lax.broadcasted_iota(jnp.int32, (8, LANES), 1)
    freq_two = signed(4 * sub + lane // 32)
    freq_three = signed(lane % 32)
    freq_line = signed(lane)
    shift_one = jnp.zeros((8, LANES), F32)
    for t in range(TRIALS):
        angle = unit * (
            freq_two * shift_smem[0, 3 * t + 1] + freq_three * shift_smem[0, 3 * t + 2]
        )
        phase_tables[0, t] = jnp.cos(angle)
        phase_tables[1, t] = jnp.sin(angle)
        shift_one = jnp.where(sub == t, shift_smem[0, 3 * t], shift_one)
    angle = unit * freq_line * shift_one
    cos_line, sin_line = jnp.cos(angle), jnp.sin(angle)
    line_tables[0] = cos_line
    line_tables[1] = sin_line
    line_tables[2] = freq_line * cos_line
    line_tables[3] = freq_line * sin_line
    line_copy = pltpu.make_async_copy(line_tables, line_smem, line_local)
    line_copy.start()

    slot_columns = 2.0 * jnp.transpose(slots)
    hot_iota = lax.broadcasted_iota(jnp.int32, (BLOCKS, SLABS * LANES), 1).astype(F32)
    for t in range(TRIALS):
        column = slot_columns[:, t : t + 1]
        hot[t, :BLOCKS, :] = jnp.where(hot_iota == column, 1.0, 0.0).astype(BF16)
        hot[t, BLOCKS:, :] = jnp.where(hot_iota == column + 1.0, 1.0, 0.0).astype(BF16)

    basis[...] = jnp.zeros((8, LANES), F32)
    for i in range(HIST):
        basis[i : i + 1, : 3 * TRIALS] = steps_ref[i]
        basis[HIST + i : HIST + i + 1, : 3 * TRIALS] = changes_ref[i]
    vectors = basis[...]
    gram = jnp.zeros((8, LANES), F32)
    for j in range(8):
        gram = jnp.where(
            lane == j, jnp.sum(vectors * vectors[j : j + 1], axis=1, keepdims=True), gram
        )
    line_copy.wait()

    def correlate(u, carry):
        for d in range(1, 8):
            peer = lax.rem(slab + d, 8)
            pltpu.make_async_remote_copy(
                src_ref=sent.at[peer, u],
                dst_ref=landed.at[peer, u],
                send_sem=data_send.at[peer, u],
                recv_sem=data_recv.at[peer, u],
                device_id=(peer, dom),
                device_id_type=MESH,
            ).wait_recv()
        for half in range(2):
            t = u + 4 * half
            arrived = landed[:, u, half * LANES : (half + 1) * LANES, :]
            box = dot(hot[t], arrived.reshape(SLABS * LANES, LANES))
            zero = jnp.zeros((8, LANES), F32)
            sum_r, sum_i, line_r, line_i, power = zero, zero, zero, zero, zero
            for k in range(EDGE):
                at = slice(8 * k, 8 * k + 8)
                box_r = box[8 * k : 8 * k + 8]
                box_i = box[BLOCKS + 8 * k : BLOCKS + 8 * k + 8]
                spec_r, spec_i, weight = weighted[0, at], weighted[1, at], weighted[2, at]
                cross_r = spec_r * box_r + spec_i * box_i
                cross_i = spec_r * box_i - spec_i * box_r
                cos_k, sin_k = line_smem[0, t, k], line_smem[1, t, k]
                cos_f, sin_f = line_smem[2, t, k], line_smem[3, t, k]
                sum_r = sum_r + (cross_r * cos_k + cross_i * sin_k)
                sum_i = sum_i + (cross_i * cos_k - cross_r * sin_k)
                line_r = line_r + (cross_r * cos_f + cross_i * sin_f)
                line_i = line_i + (cross_i * cos_f - cross_r * sin_f)
                power = power + weight * (box_r * box_r + box_i * box_i)
            cos_t, sin_t = phase_tables[0, t], phase_tables[1, t]
            real = sum_r * cos_t + sum_i * sin_t
            imag = sum_i * cos_t - sum_r * sin_t
            imag_one = line_i * cos_t - line_r * sin_t
            for n, tile in enumerate(
                (real, imag_one, imag * freq_two, imag * freq_three, power)
            ):
                partial[n, pl.ds(t, 1), :] = jnp.sum(tile, axis=0, keepdims=True)
        return carry

    lax.fori_loop(0, 4, correlate, 0)

    totals = [jnp.sum(partial[n], axis=1, keepdims=True) for n in range(5)]
    factor = math.sqrt(EDGE**3) / jnp.sqrt((power_particle + 1e-06) * (totals[4] + 1e-06))
    scores = jnp.sum(jnp.where(lane == sub, factor * totals[0], 0.0), axis=0, keepdims=True)
    scores_ref[...] = scores[:, :TRIALS]
    active = (1 - flag_ref[0]).astype(F32)
    place = lane - 3 * sub
    slopes = jnp.where(place == 0, totals[1], 0.0)
    slopes = jnp.where(place == 1, totals[2], slopes)
    slopes = jnp.where(place == 2, totals[3], slopes)
    gradient = jnp.sum(-active * (factor * unit) * slopes, axis=0, keepdims=True)
    gram = jnp.where(lane == 8, jnp.sum(vectors * gradient, axis=1, keepdims=True), gram)

    stages = (
        (slab_peers, sum_slab, slab, 0, lambda d: lax.rem(slab + d, 8)),
        (z_peers, sum_z, z_at, 7, lambda d: lax.rem(z_at + d, 8)),
        (x_peers, sum_x, x_at, 14, lambda d: lax.rem(x_at + d, 4)),
    )
    for number, (peers, buffer, own, start, index_of) in enumerate(stages):
        sum_out[number] = gram
        buffer[own] = gram
        size = len(peers) + 1
        for d in range(1, size):
            pltpu.make_async_remote_copy(
                src_ref=sum_out.at[number],
                dst_ref=buffer.at[own],
                send_sem=sum_send.at[start + d - 1],
                recv_sem=sum_recv.at[start + d - 1],
                device_id=peers[d - 1],
                device_id_type=MESH,
            ).start()
        for d in range(1, size):
            pltpu.make_async_remote_copy(
                src_ref=sum_out.at[number],
                dst_ref=buffer.at[index_of(size - d)],
                send_sem=sum_send.at[start + d - 1],
                recv_sem=sum_recv.at[start + d - 1],
                device_id=peers[d - 1],
                device_id_type=MESH,
            ).wait_recv()
        gram = jnp.sum(buffer[...], axis=0)

    lane_row = lane[:1]
    held = jnp.where(lane_row == 2 * HIST, 1.0, 0.0)
    curvature = [gram[i : i + 1, HIST + i : HIST + i + 1] for i in range(HIST)]
    alphas = [None] * HIST
    for i in reversed(range(HIST)):
        alphas[i] = jnp.sum(gram[i : i + 1] * held, axis=1, keepdims=True) / curvature[i]
        held = jnp.where(lane_row == HIST + i, held - alphas[i], held)
    last = 2 * HIST - 1
    gamma = curvature[HIST - 1] / gram[last : last + 1, last : last + 1]
    held = gamma * held
    direction = gradient
    for i in range(HIST):
        direction = direction - alphas[i] * vectors[HIST + i : HIST + i + 1]
    direction = gamma * direction
    for i in range(HIST):
        beta = (
            jnp.sum(gram[HIST + i : HIST + i + 1] * held, axis=1, keepdims=True)
            / curvature[i]
        )
        held = jnp.where(lane_row == i, held + (alphas[i] - beta), held)
        direction = direction + (alphas[i] - beta) * vectors[i : i + 1]
    new_ref[...] = shift_ref[...] - active * direction[:, : 3 * TRIALS]

    for d in range(1, 8):
        ask(lax.rem(slab + d, 8)).wait_send()

    def drain(u, carry):
        for d in range(1, 8):
            data(lax.rem(slab + d, 8), u).wait_send()
        return carry

    lax.fori_loop(0, 4, drain, 0)
    for number, (peers, buffer, own, start, index_of) in enumerate(stages):
        for d in range(1, len(peers) + 1):
            pltpu.make_async_remote_copy(
                src_ref=sum_out.at[number],
                dst_ref=buffer.at[own],
                send_sem=sum_send.at[start + d - 1],
                recv_sem=sum_recv.at[start + d - 1],
                device_id=peers[d - 1],
                device_id_type=MESH,
            ).wait_send()


def local(
    reference_blocks,
    corner_maps,
    volumes,
    wedge,
    source_slab,
    block_offset,
    flags,
    shifts,
    past_steps,
    past_changes,
):
    row_count = reference_blocks.shape[0] * 2
    inner_pair, outer_pair, twiddle = transform_tables()
    vmem = pl.BlockSpec(memory_space=pltpu.VMEM)
    smem = pl.BlockSpec(memory_space=pltpu.SMEM)
    dma = pltpu.SemaphoreType.DMA
    return pl.pallas_call(
        step_kernel,
        out_shape=(
            jax.ShapeDtypeStruct((1, TRIALS), F32),
            jax.ShapeDtypeStruct((1, 3 * TRIALS), F32),
        ),
        in_specs=[vmem] * 6 + [smem, smem] + [vmem] * 6,
        out_specs=(vmem, vmem),
        scratch_shapes=[
            pltpu.VMEM((row_count + 16, LANES), F32),
            pltpu.VMEM((SLABS, 8, LANES), jnp.int32),
            pltpu.VMEM((SLABS, 8, LANES), jnp.int32),
            pltpu.SMEM((SLABS, 8, LANES), jnp.int32),
            pltpu.VMEM((2 * LANES, LANES), F32),
            pltpu.VMEM((SLABS, 4, 2 * LANES, LANES), BF16),
            pltpu.VMEM((SLABS, 4, 2 * LANES, LANES), BF16),
            pltpu.VMEM((TRIALS, 2 * BLOCKS, SLABS * LANES), BF16),
            pltpu.VMEM((3, BLOCKS, LANES), F32),
            pltpu.VMEM((2, TRIALS, 8, LANES), F32),
            pltpu.VMEM((4, TRIALS, LANES), F32),
            pltpu.SMEM((4, TRIALS, LANES), F32),
            pltpu.VMEM((5, TRIALS, LANES), F32),
            pltpu.VMEM((8, LANES), F32),
            pltpu.VMEM((8, 8, LANES), F32),
            pltpu.VMEM((8, 8, LANES), F32),
            pltpu.VMEM((4, 8, LANES), F32),
            pltpu.VMEM((3, 8, LANES), F32),
            dma((8,)),
            dma((8,)),
            dma,
            dma((8, 4)),
            dma((8, 4)),
            dma,
            dma((17,)),
            dma((17,)),
        ],
        compiler_params=pltpu.CompilerParams(
            collective_id=0, has_side_effects=True, vmem_limit_bytes=56 * 2**20
        ),
    )(
        reference_blocks.reshape(row_count, LANES),
        corner_maps,
        volumes,
        wedge.reshape(BLOCKS, LANES),
        source_slab.reshape(TRIALS, 1, BLOCKS),
        block_offset.reshape(TRIALS, BLOCKS),
        flags,
        shifts,
        shifts,
        past_steps,
        past_changes,
        jnp.asarray(inner_pair),
        jnp.asarray(outer_pair),
        jnp.asarray(twiddle),
    )


def solution(mesh):
    return jax.shard_map(
        local,
        mesh=mesh,
        in_specs=(
            P("slab", None, None),
            P(),
            P(("slab", "dom"), None, None, None),
            P(("slab", "dom"), None),
            P(("slab", "dom"), None, None, None),
            P(("slab", "dom"), None, None),
            P(("slab", "dom")),
            P(("slab", "dom"), None),
            P(None, ("slab", "dom"), None),
            P(None, ("slab", "dom"), None),
        ),
        out_specs=(P(("slab", "dom"), None), P(("slab", "dom"), None)),
        check_vma=False,
    )
```

time: 944 us -> 63 us (0.07)
  blocking collectives: 593 us -> 0 us
  waiting for transfers between devices: 129 us -> 0 us
  local copies, waits for them, and re-layouts: 127 us -> 2.25 us
  Pallas kernels: 0 us -> 59.3 us
  other arithmetic: 54.6 us -> 0 us
  between operations: 27.7 us -> 1.29 us
  matrix products: 10.8 us -> 0 us
    psum x8 -> x0, blocking collectives: 593 us -> none  [the longest x4 298 us: local(): lax.psum(jnp.sum(past_steps[pair] * direction), ('slab', 'dom'))]
    all_gather x1 -> x0, waiting for transfers between devices: 128 us -> none  [local(): shard_piece = lax.all_gather(reference_blocks, 'slab', axis=0, tiled=True)]
    gather x1 -> x0, local copies, waits for them, and re-layouts: 115 us -> none  [local(): jnp.take(shard_piece, jnp.clip(wanted_rows, 0, piece_rows - 1), axis=0)]
    pallas_call x0 -> x1, Pallas kernels: none -> 59.3 us  [local(): pl.pallas_call(step_kernel, out_shape=(jax.ShapeDtypeStruct((1, TRIALS),...]
    select_n x2 -> x0, other arithmetic: 41.6 us -> none  [the longest x1 41.5 us: local(): jnp.where(inside[..., None, None], taken, jnp.zeros_like(taken))]
    reduce_sum x11 -> x0, other arithmetic: 11 us -> none  [the longest x1 5.15 us: pose_terms(): jnp.sum(wedge_weight * (box_real * box_real + box_imag * box_imag), axis=-1)]
    dot_general x18 -> x0, matrix products: 10.8 us -> none  [the longest x8 3.34 us: local(): jnp.dot(picked_all[corner].reshape(-1, 128), corner_maps[corner], preferr...]
  transfers between devices with their start and end apart: 1 -> 0, of which waited for: 1 -> 0; matrix products, arithmetic and copies ran while one was open for 1% -> 0% of each run, Pallas kernels for 0% -> 0%
where the time goes in v2:
time: 63 us; the launch traced here: 62.9 us
  Pallas kernels  59.3 us (94%)
  local copies, waits for them, and re-layouts  2.25 us (4%)
  between operations  1.29 us (2%)
    pallas_call x1, Pallas kernels, local(): pl.pallas_call(step_kernel, out_shape=(jax.ShapeDtypeStruct((1, TRIALS),...  59.3 us
    unnamed x2, local copies, waits for them, and re-layouts  2.25 us

profile of v2, /device:TPU:1, one launch (start us, length us, event | category | flops | bytes accessed | tf_op | source)
XLA Modules:
  0.0 62.9 jit_solution(15705199661329417692)
XLA Ops:
  1.3 59.3 %shard_map.140 = (f32[1,8]{1,0:T(1,128)}, f32[1,24]{1,0:T(1,128)}) custom-call(bf16[13824,128]{1,0:T(8,128)(2,1)} %bitcast.4, bf16[8,128,128]{2,1,0:T(8,128)(2,1)} %maps_ref.1, bf16[1,32,32,32]{3,2,1,0:T(8,128)(2,1)} %volume_ref.1, s32[256,128]{1,0:T(8,128)} %bitcast.5, s32[8,1,256]{2,1,0:T(1,128)} %bitcast.6, s32[8,256]{1,0:T(8,128)} %bitcast.7, ...), custom_call_target="tpu_custom_call" | custom-call | tf_op jit(solution)/shard_map/pallas_call | solution.py:464
  60.6 1.1 %copy.18 = f32[1,8]{1,0:T(1,128)} copy(f32[1,8]{1,0:T(1,128)} %get-tuple-element.4) | data formatting | bytes 64
  61.7 1.1 %copy.19 = f32[1,24]{1,0:T(1,128)} copy(f32[1,24]{1,0:T(1,128)} %get-tuple-element.5) | data formatting | bytes 192

commit v3 on v2

--- a/solution.py
+++ b/solution.py
@@ -17,8 +17,10 @@
 BLOCKS = 256
 LANES = 128
 SLABS = 8
+NEAR = 6
 MESH = pl.DeviceIdType.MESH
 CHUNK = 768
+FIRST_CHUNKS = 3
 F32 = jnp.float32
 BF16 = jnp.bfloat16
 
@@ -63,27 +65,45 @@
 
 
 def step_kernel(
+    rows_hbm,
+    maps_hbm,
+    volume_hbm,
+    wedge_hbm,
+    slab_hbm,
+    offset_hbm,
+    steps_hbm,
+    changes_hbm,
+    inner_hbm,
+    outer_hbm,
+    twiddle_hbm,
+    flag_ref,
+    shift_smem,
+    shift_ref,
+    scores_ref,
+    new_ref,
     rows_ref,
     maps_ref,
     volume_ref,
     wedge_ref,
     slab_ref,
     offset_ref,
-    flag_ref,
-    shift_smem,
-    shift_ref,
     steps_ref,
     changes_ref,
     inner_ref,
     outer_ref,
     twiddle_ref,
-    scores_ref,
-    new_ref,
     mapped,
     asked_out,
     asked_in,
     asked_smem,
     staged,
+    kept,
+    side_out,
+    side_in,
+    info_out,
+    info_in,
+    part_out,
+    part_in,
     sent,
     landed,
     hot,
@@ -97,11 +117,15 @@
     sum_z,
     sum_x,
     sum_out,
+    load_sem,
     ask_send,
     ask_recv,
     ask_local,
     data_send,
     data_recv,
+    side_sem,
+    info_sem,
+    part_sem,
     line_local,
     sum_send,
     sum_recv,
@@ -109,6 +133,18 @@
     slab = lax.axis_index("slab")
     dom = lax.axis_index("dom")
     z_at, x_at = dom // 4, lax.rem(dom, 4)
+    y_at, core = slab // 2, lax.rem(slab, 2)
+    near_steps = (1, 2, 6, 7, 3 + 2 * core)
+    far = (lax.rem(slab + 4, 8), lax.rem(slab + 5 - 2 * core, 8))
+
+    def place_at(peer):
+        step = lax.rem(y_at - peer // 2 + 4, 4)
+        return (step - step // 3) * 2 + core
+
+    def place_of(peer):
+        step = lax.rem(peer // 2 - y_at + 4, 4)
+        return (step - step // 3) * 2 + lax.rem(peer, 2)
+
     slab_peers = [(lax.rem(slab + d, 8), dom) for d in range(1, 8)]
     z_peers = [(slab, lax.rem(z_at + d, 8) * 4 + x_at) for d in range(1, 8)]
     x_peers = [(slab, z_at * 4 + lax.rem(x_at + d, 4)) for d in range(1, 4)]
@@ -116,6 +152,28 @@
     barrier = pltpu.get_barrier_semaphore()
     for peer in slab_peers + z_peers + x_peers:
         pl.semaphore_signal(barrier, inc=1, device_id=peer, device_id_type=MESH)
+
+    pairs = (
+        (slab_hbm, slab_ref),
+        (offset_hbm, offset_ref),
+        (maps_hbm, maps_ref),
+        (rows_hbm, rows_ref),
+        (volume_hbm, volume_ref),
+        (inner_hbm, inner_ref),
+        (outer_hbm, outer_ref),
+        (twiddle_hbm, twiddle_ref),
+        (wedge_hbm, wedge_ref),
+        (steps_hbm, steps_ref),
+        (changes_hbm, changes_ref),
+    )
+    loads = [
+        pltpu.make_async_copy(source, target, load_sem.at[n])
+        for n, (source, target) in enumerate(pairs)
+    ]
+    for load in loads:
+        load.start()
+    loads[0].wait()
+    loads[1].wait()
 
     slab_rows = [slab_ref[t] for t in range(TRIALS)]
     slab_iota = lax.broadcasted_iota(jnp.int32, (SLABS, BLOCKS), 0)
@@ -136,28 +194,78 @@
     )
     offsets = offset_ref[...]
     high = offsets // LANES
-    digits = jnp.concatenate([high, offsets - high * LANES], axis=0).astype(F32).astype(BF16)
+    numbers = lax.broadcasted_iota(jnp.int32, (TRIALS, BLOCKS), 1) + 1
+    digits = (
+        jnp.concatenate([high, offsets - high * LANES, numbers], axis=0)
+        .astype(F32)
+        .astype(BF16)
+    )
     slot_iota = lax.broadcasted_iota(jnp.int32, (SLABS * CAP, BLOCKS), 0).astype(F32)
     trial_iota = lax.broadcasted_iota(jnp.int32, (TRIALS, SLABS * CAP), 0)
     asked = jnp.zeros((TRIALS, SLABS * CAP), F32)
+    listed = asked
     for t in range(TRIALS):
         placed = jnp.where(slot_iota == slots[t : t + 1], 1.0, 0.0).astype(BF16)
         found = lax.dot_general(
             digits, placed, (((1,), (1,)), ((), ())), preferred_element_type=F32
         )
         asked = jnp.where(
-            trial_iota == t, found[:TRIALS] * LANES + found[TRIALS:], asked
-        )
+            trial_iota == t, found[:TRIALS] * LANES + found[TRIALS : 2 * TRIALS], asked
+        )
+        listed = jnp.where(trial_iota == t, found[2 * TRIALS :], listed)
     asked = asked.astype(jnp.int32) * 2 + 8
     lane4 = lax.broadcasted_iota(jnp.int32, (4, LANES), 1)
-    for s in range(SLABS):
-        tile = asked[:, (s // 2) * LANES : (s // 2 + 1) * LANES]
+    listed = listed.astype(jnp.int32)
+
+    def slab_lanes(table, s):
+        tile = table[:, (s // 2) * LANES : (s // 2 + 1) * LANES]
         turned = pltpu.roll(tile, CAP, 1)
         if s % 2 == 0:
-            both = jnp.where(lane4 < CAP, tile[:4], turned[4:])
-        else:
-            both = jnp.where(lane4 < CAP, turned[:4], tile[4:])
-        asked_out[s] = jnp.concatenate([both, jnp.zeros((4, LANES), jnp.int32)], axis=0)
+            return jnp.where(lane4 < CAP, tile[:4], turned[4:])
+        return jnp.where(lane4 < CAP, turned[:4], tile[4:])
+
+    for s in range(SLABS):
+        asked_out[s] = jnp.concatenate([slab_lanes(asked, s), slab_lanes(listed, s)], axis=0)
+
+    sub = lax.broadcasted_iota(jnp.int32, (8, LANES), 0)
+    lane = lax.broadcasted_iota(jnp.int32, (8, LANES), 1)
+    own_shifts = jnp.zeros((8, LANES), F32)
+    for t in range(TRIALS):
+        for a in range(3):
+            own_shifts = jnp.where(
+                (sub == t) & (lane == a), shift_smem[0, 3 * t + a], own_shifts
+            )
+    side_out[...] = own_shifts
+    loads[4].wait()
+    loads[8].wait()
+    volume = volume_ref[0].astype(F32)
+    info_out[:BLOCKS, :] = jnp.concatenate(
+        [volume[:, 8 * g : 8 * g + 8, :].reshape(BLOCKS, EDGE) for g in range(4)], axis=1
+    ).astype(BF16)
+    info_out[BLOCKS:, :] = wedge_ref[...].astype(F32).astype(BF16)
+
+    loads[2].wait()
+    loads[3].wait()
+
+    maps = jnp.concatenate(
+        [maps_ref[:4].reshape(512, LANES), maps_ref[4:].reshape(512, LANES)], axis=1
+    )
+    row_count = rows_ref.shape[0]
+
+    def map_chunk(base, rows):
+        wide = jnp.concatenate([rows[2 * m : 2 * m + CHUNK] for m in range(4)], axis=1)
+        both = dot(wide, maps)
+        mapped[pl.ds(pl.multiple_of(base + 8, 8), CHUNK), :] = both[:, :LANES]
+        mapped[pl.ds(pl.multiple_of(base, 8), CHUNK), :] += both[:, LANES:]
+
+    mapped[0:8, :] = jnp.zeros((8, LANES), F32)
+
+    def map_step(i, carry):
+        base = pl.multiple_of(i * CHUNK, CHUNK)
+        map_chunk(base, rows_ref[pl.ds(base, CHUNK + 16), :])
+        return carry
+
+    lax.fori_loop(0, FIRST_CHUNKS, map_step, 0)
 
     pl.semaphore_wait(barrier, 17)
 
@@ -173,32 +281,30 @@
 
     for d in range(1, 8):
         ask(lax.rem(slab + d, 8)).start()
-    asked_in[slab] = asked_out[slab]
-
-    maps = jnp.concatenate(
-        [maps_ref[:4].reshape(512, LANES), maps_ref[4:].reshape(512, LANES)], axis=1
-    )
-    row_count = rows_ref.shape[0]
-
-    def map_chunk(base, rows):
-        wide = jnp.concatenate([rows[2 * m : 2 * m + CHUNK] for m in range(4)], axis=1)
-        both = dot(wide, maps)
-        mapped[pl.ds(pl.multiple_of(base + 8, 8), CHUNK), :] = both[:, :LANES]
-        mapped[pl.ds(pl.multiple_of(base, 8), CHUNK), :] += both[:, LANES:]
-
-    mapped[0:8, :] = jnp.zeros((8, LANES), F32)
-
-    def map_step(i, carry):
-        base = pl.multiple_of(i * CHUNK, CHUNK)
-        map_chunk(base, rows_ref[pl.ds(base, CHUNK + 16), :])
-        return carry
-
-    lax.fori_loop(0, row_count // CHUNK - 1, map_step, 0)
+
+    def far_copy(source, target, sems, which):
+        return pltpu.make_async_remote_copy(
+            src_ref=source,
+            dst_ref=target.at[which],
+            send_sem=sems.at[0, which],
+            recv_sem=sems.at[1, which],
+            device_id=(far[which], dom),
+            device_id_type=MESH,
+        )
+
+    for which in range(2):
+        far_copy(side_out, side_in, side_sem, which).start()
+        far_copy(info_out, info_in, info_sem, which).start()
+
+    lax.fori_loop(FIRST_CHUNKS, row_count // CHUNK - 1, map_step, 0)
     map_chunk(
         row_count - CHUNK,
         jnp.concatenate([rows_ref[row_count - CHUNK :, :], rows_ref[:16, :]], axis=0),
     )
     mapped[row_count : row_count + 8, :] += mapped[0:8, :]
+
+    def to_smem(source, peer):
+        return pltpu.make_async_copy(source, asked_smem.at[peer], ask_local.at[peer])
 
     for d in range(1, 8):
         peer = lax.rem(slab + d, 8)
@@ -210,60 +316,82 @@
             device_id=(peer, dom),
             device_id_type=MESH,
         ).wait_recv()
-    to_smem = pltpu.make_async_copy(asked_in, asked_smem, ask_local)
-    to_smem.start()
-    to_smem.wait()
+        to_smem(asked_in.at[peer], peer).start()
+    to_smem(asked_out.at[slab], slab).start()
+    for d in range(1, 8):
+        peer = lax.rem(slab + d, 8)
+        to_smem(asked_in.at[peer], peer).wait()
+    to_smem(asked_out.at[slab], slab).wait()
 
     def data(peer, u):
         return pltpu.make_async_remote_copy(
             src_ref=sent.at[peer, u],
-            dst_ref=landed.at[slab, u],
+            dst_ref=landed.at[place_at(peer), u],
             send_sem=data_send.at[peer, u],
-            recv_sem=data_recv.at[slab, u],
+            recv_sem=data_recv.at[place_at(peer), u],
             device_id=(peer, dom),
             device_id_type=MESH,
         )
 
-    def pick(peer, u):
+    def pick(peer, u, target):
         for j in range(LANES):
             place = jnp.minimum(jnp.maximum(asked_smem[peer, u, j], 8), row_count + 6)
-            staged[2 * j : 2 * j + 2, :] = mapped[pl.ds(place, 2), :]
-        return staged[...].astype(BF16)
+            target[2 * j : 2 * j + 2, :] = mapped[pl.ds(place, 2), :]
 
     def pick_trials(u, carry):
-        def pick_peer(d, inner):
-            peer = lax.rem(slab + d, 8)
-            sent[peer, u] = pick(peer, u)
+        def pick_peer(n, inner):
+            step = n + 1 + 3 * (n // 2) - (n // 4) * (8 - 2 * core)
+            peer = lax.rem(slab + step, 8)
+            pick(peer, u, staged)
+            sent[peer, u] = staged[...].astype(BF16)
             data(peer, u).start()
             return inner
 
-        lax.fori_loop(1, 8, pick_peer, 0)
-        landed[slab, u] = pick(slab, u)
+        lax.fori_loop(0, 5, pick_peer, 0)
         return carry
 
     lax.fori_loop(0, 4, pick_trials, 0)
 
-    volume = volume_ref[0].astype(F32)
-    first = jnp.zeros((BLOCKS, 2 * LANES), F32)
-    for g in range(4):
-        part = volume[:, 8 * g : 8 * g + 8, :].reshape(BLOCKS, EDGE).astype(BF16)
-        first = first + dot(part, inner_ref[0, 32 * g : 32 * g + 32, :])
-        first = first + dot(part, inner_ref[1, 32 * g : 32 * g + 32, :])
-    first = first.reshape(EDGE, 8, 2 * LANES)
-    first_r, first_i = first[:, :, :LANES], first[:, :, LANES:]
+    def pick_own(u, carry):
+        pick(slab, u, staged)
+        landed[core, u] = staged[...].astype(BF16)
+        return carry
+
+    lax.fori_loop(0, 4, pick_own, 0)
+
+    def pick_far(n, carry):
+        which, u = n // 4, lax.rem(n, 4)
+        pick(lax.rem(slab + 4 + which * (1 - 2 * core), 8), u, kept.at[which, u])
+        return carry
+
+    lax.fori_loop(0, 8, pick_far, 0)
+
+    for n in (5, 6, 7, 9, 10):
+        loads[n].wait()
+
     turn_r, turn_i = twiddle_ref[0][None], twiddle_ref[1][None]
-    second = jnp.concatenate(
-        [first_r * turn_r - first_i * turn_i, first_r * turn_i + first_i * turn_r], axis=-1
-    ).reshape(BLOCKS, 2 * LANES)
-    second_high = second.astype(BF16)
-    second_low = (second - second_high.astype(F32)).astype(BF16)
-    third = (
-        dot(outer_ref[0], second_high)
-        + dot(outer_ref[0], second_low)
-        + dot(outer_ref[1], second_high)
-    )
-    spec_r = third[:BLOCKS, :LANES] - third[BLOCKS:, LANES:]
-    spec_i = third[:BLOCKS, LANES:] + third[BLOCKS:, :LANES]
+
+    def spectrum(volume_rows):
+        first = dot(volume_rows, inner_ref[0]) + dot(volume_rows, inner_ref[1])
+        first = first.reshape(EDGE, 8, 2 * LANES)
+        first_r, first_i = first[:, :, :LANES], first[:, :, LANES:]
+        second = jnp.concatenate(
+            [first_r * turn_r - first_i * turn_i, first_r * turn_i + first_i * turn_r],
+            axis=-1,
+        ).reshape(BLOCKS, 2 * LANES)
+        second_high = second.astype(BF16)
+        second_low = (second - second_high.astype(F32)).astype(BF16)
+        third = (
+            dot(outer_ref[0], second_high)
+            + dot(outer_ref[0], second_low)
+            + dot(outer_ref[1], second_high)
+        )
+        return (
+            third[:BLOCKS, :LANES] - third[BLOCKS:, LANES:],
+            third[:BLOCKS, LANES:] + third[BLOCKS:, :LANES],
+        )
+
+    spec_r, spec_i = spectrum(info_out[:BLOCKS, :])
     weight = wedge_ref[...].astype(F32)
     weighted[0] = weight * spec_r
     weighted[1] = weight * spec_i
@@ -275,8 +403,6 @@
     )
 
     unit = 2.0 * math.pi / EDGE
-    sub = lax.broadcasted_iota(jnp.int32, (8, LANES), 0)
-    lane = lax.broadcasted_iota(jnp.int32, (8, LANES), 1)
     freq_two = signed(4 * sub + lane // 32)
     freq_three = signed(lane % 32)
     freq_line = signed(lane)
@@ -297,8 +423,14 @@
     line_copy = pltpu.make_async_copy(line_tables, line_smem, line_local)
     line_copy.start()
 
-    slot_columns = 2.0 * jnp.transpose(slots)
-    hot_iota = lax.broadcasted_iota(jnp.int32, (BLOCKS, SLABS * LANES), 1).astype(F32)
+    place_rows = []
+    for t in range(TRIALS):
+        step = (slab_rows[t] // 2 - y_at + 4) % 4
+        near = jnp.where(step == 3, 2, step) * 2 + slab_rows[t] % 2
+        near = jnp.where(step == 2, -2 * SLABS, near - slab_rows[t])
+        place_rows.append(slots[t : t + 1] + (CAP * near).astype(F32))
+    slot_columns = 2.0 * jnp.transpose(jnp.concatenate(place_rows, axis=0))
+    hot_iota = lax.broadcasted_iota(jnp.int32, (BLOCKS, NEAR * LANES), 1).astype(F32)
     for t in range(TRIALS):
         column = slot_columns[:, t : t + 1]
         hot[t, :BLOCKS, :] = jnp.where(hot_iota == column, 1.0, 0.0).astype(BF16)
@@ -314,23 +446,85 @@
         gram = jnp.where(
             lane == j, jnp.sum(vectors * vectors[j : j + 1], axis=1, keepdims=True), gram
         )
+
+    block_iota = lax.broadcasted_iota(jnp.int32, (LANES, BLOCKS), 1).astype(F32)
+    slot_lane = lax.broadcasted_iota(jnp.int32, (LANES, LANES), 1)
+    slot_first = lax.broadcasted_iota(jnp.int32, (LANES, 1), 0) < CAP
+    slot_three = signed(slot_lane % 32)
+    for which in range(2):
+        far_copy(side_out, side_in, side_sem, which).wait_recv()
+        far_copy(info_out, info_in, info_sem, which).wait_recv()
+        far_r, far_i = spectrum(info_in[which, :BLOCKS, :])
+        far_weight = info_in[which, BLOCKS:, :]
+        far_r, far_i = far_r * far_weight.astype(F32), far_i * far_weight.astype(F32)
+        high_r, high_i = far_r.astype(BF16), far_i.astype(BF16)
+        packed = jnp.concatenate(
+            [
+                high_r,
+                high_i,
+                (far_r - high_r.astype(F32)).astype(BF16),
+                (far_i - high_i.astype(F32)).astype(BF16),
+                far_weight,
+            ],
+            axis=1,
+        )
+        far_columns = jnp.transpose(asked_in[far[which]].astype(F32)) - 1.0
+        far_shifts = side_in[which]
+        for u in range(4):
+            column = far_columns[:, 4 + u : 5 + u]
+            chosen = dot(jnp.where(block_iota == column, 1.0, 0.0).astype(BF16), packed)
+            slot_r = chosen[:, :LANES] + chosen[:, 2 * LANES : 3 * LANES]
+            slot_i = chosen[:, LANES : 2 * LANES] + chosen[:, 3 * LANES : 4 * LANES]
+            slot_weight = chosen[:, 4 * LANES :]
+            block = jnp.maximum(column, 0.0).astype(jnp.int32)
+            slot_one = signed(block // 8)
+            slot_two = signed(4 * (block % 8) + slot_lane // 32)
+            trio = [
+                jnp.where(
+                    slot_first, far_shifts[u : u + 1, a : a + 1], far_shifts[u + 4 : u + 5, a : a + 1]
+                )
+                for a in range(3)
+            ]
+            angle = unit * (slot_one * trio[0] + slot_two * trio[1] + slot_three * trio[2])
+            cos_s, sin_s = jnp.cos(angle), jnp.sin(angle)
+            row_r = kept[which, u, pl.ds(0, LANES, stride=2), :].astype(BF16).astype(F32)
+            row_i = kept[which, u, pl.ds(1, LANES, stride=2), :].astype(BF16).astype(F32)
+            cross_r = slot_r * row_r + slot_i * row_i
+            cross_i = slot_r * row_i - slot_i * row_r
+            real = cross_r * cos_s + cross_i * sin_s
+            imag = cross_i * cos_s - cross_r * sin_s
+            power = slot_weight * (row_r * row_r + row_i * row_i)
+            for n, tile in enumerate(
+                (real, imag * slot_one, imag * slot_two, imag * slot_three, power)
+            ):
+                for half in range(2):
+                    t = u + 4 * half
+                    partial[n, t : t + 1, :] = jnp.sum(
+                        tile[half * CAP : (half + 1) * CAP], axis=0, keepdims=True
+                    )
+        tile = jnp.zeros((8, LANES), F32)
+        for n in range(5):
+            tile = jnp.where(lane == n, jnp.sum(partial[n], axis=1, keepdims=True), tile)
+        part_out[which] = tile
+        far_copy(part_out.at[which], part_in, part_sem, which).start()
+
     line_copy.wait()
 
     def correlate(u, carry):
-        for d in range(1, 8):
+        for d in near_steps:
             peer = lax.rem(slab + d, 8)
             pltpu.make_async_remote_copy(
                 src_ref=sent.at[peer, u],
-                dst_ref=landed.at[peer, u],
+                dst_ref=landed.at[place_of(peer), u],
                 send_sem=data_send.at[peer, u],
-                recv_sem=data_recv.at[peer, u],
+                recv_sem=data_recv.at[place_of(peer), u],
                 device_id=(peer, dom),
                 device_id_type=MESH,
             ).wait_recv()
         for half in range(2):
             t = u + 4 * half
             arrived = landed[:, u, half * LANES : (half + 1) * LANES, :]
-            box = dot(hot[t], arrived.reshape(SLABS * LANES, LANES))
+            box = dot(hot[t], arrived.reshape(NEAR * LANES, LANES))
             zero = jnp.zeros((8, LANES), F32)
             sum_r, sum_i, line_r, line_i, power = zero, zero, zero, zero, zero
             for k in range(EDGE):
@@ -359,7 +553,12 @@
 
     lax.fori_loop(0, 4, correlate, 0)
 
-    totals = [jnp.sum(partial[n], axis=1, keepdims=True) for n in range(5)]
+    for which in range(2):
+        far_copy(part_out.at[which], part_in, part_sem, which).wait_recv()
+    far_part = part_in[0] + part_in[1]
+    totals = [
+        jnp.sum(partial[n], axis=1, keepdims=True) + far_part[:, n : n + 1] for n in range(5)
+    ]
     factor = math.sqrt(EDGE**3) / jnp.sqrt((power_particle + 1e-06) * (totals[4] + 1e-06))
     scores = jnp.sum(jnp.where(lane == sub, factor * totals[0], 0.0), axis=0, keepdims=True)
     scores_ref[...] = scores[:, :TRIALS]
@@ -426,8 +625,13 @@
     for d in range(1, 8):
         ask(lax.rem(slab + d, 8)).wait_send()
 
+    for which in range(2):
+        far_copy(side_out, side_in, side_sem, which).wait_send()
+        far_copy(info_out, info_in, info_sem, which).wait_send()
+        far_copy(part_out.at[which], part_in, part_sem, which).wait_send()
+
     def drain(u, carry):
-        for d in range(1, 8):
+        for d in near_steps:
             data(lax.rem(slab + d, 8), u).wait_send()
         return carry
 
@@ -460,24 +664,46 @@
     inner_pair, outer_pair, twiddle = transform_tables()
     vmem = pl.BlockSpec(memory_space=pltpu.VMEM)
     smem = pl.BlockSpec(memory_space=pltpu.SMEM)
+    hbm = pl.BlockSpec(memory_space=pl.ANY)
     dma = pltpu.SemaphoreType.DMA
+    large = (
+        reference_blocks.reshape(row_count, LANES),
+        corner_maps,
+        volumes,
+        wedge.reshape(BLOCKS, LANES),
+        source_slab.reshape(TRIALS, 1, BLOCKS),
+        block_offset.reshape(TRIALS, BLOCKS),
+        past_steps,
+        past_changes,
+        jnp.asarray(inner_pair),
+        jnp.asarray(outer_pair),
+        jnp.asarray(twiddle),
+    )
     return pl.pallas_call(
         step_kernel,
         out_shape=(
             jax.ShapeDtypeStruct((1, TRIALS), F32),
             jax.ShapeDtypeStruct((1, 3 * TRIALS), F32),
         ),
-        in_specs=[vmem] * 6 + [smem, smem] + [vmem] * 6,
+        in_specs=[hbm] * len(large) + [smem, smem, vmem],
         out_specs=(vmem, vmem),
-        scratch_shapes=[
+        scratch_shapes=[pltpu.VMEM(a.shape, a.dtype) for a in large]
+        + [
             pltpu.VMEM((row_count + 16, LANES), F32),
             pltpu.VMEM((SLABS, 8, LANES), jnp.int32),
             pltpu.VMEM((SLABS, 8, LANES), jnp.int32),
             pltpu.SMEM((SLABS, 8, LANES), jnp.int32),
             pltpu.VMEM((2 * LANES, LANES), F32),
+            pltpu.VMEM((2, 4, 2 * LANES, LANES), F32),
+            pltpu.VMEM((8, LANES), F32),
+            pltpu.VMEM((2, 8, LANES), F32),
+            pltpu.VMEM((2 * BLOCKS, LANES), BF16),
+            pltpu.VMEM((2, 2 * BLOCKS, LANES), BF16),
+            pltpu.VMEM((2, 8, LANES), F32),
+            pltpu.VMEM((2, 8, LANES), F32),
             pltpu.VMEM((SLABS, 4, 2 * LANES, LANES), BF16),
-            pltpu.VMEM((SLABS, 4, 2 * LANES, LANES), BF16),
-            pltpu.VMEM((TRIALS, 2 * BLOCKS, SLABS * LANES), BF16),
+            pltpu.VMEM((NEAR, 4, 2 * LANES, LANES), BF16),
+            pltpu.VMEM((TRIALS, 2 * BLOCKS, NEAR * LANES), BF16),
             pltpu.VMEM((3, BLOCKS, LANES), F32),
             pltpu.VMEM((2, TRIALS, 8, LANES), F32),
             pltpu.VMEM((4, TRIALS, LANES), F32),
@@ -488,11 +714,15 @@
             pltpu.VMEM((8, 8, LANES), F32),
             pltpu.VMEM((4, 8, LANES), F32),
             pltpu.VMEM((3, 8, LANES), F32),
+            dma((11,)),
             dma((8,)),
             dma((8,)),
-            dma,
+            dma((8,)),
             dma((8, 4)),
-            dma((8, 4)),
+            dma((NEAR, 4)),
+            dma((2, 2)),
+            dma((2, 2)),
+            dma((2, 2)),
             dma,
             dma((17,)),
             dma((17,)),
@@ -500,22 +730,7 @@
         compiler_params=pltpu.CompilerParams(
             collective_id=0, has_side_effects=True, vmem_limit_bytes=56 * 2**20
         ),
-    )(
-        reference_blocks.reshape(row_count, LANES),
-        corner_maps,
-        volumes,
-        wedge.reshape(BLOCKS, LANES),
-        source_slab.reshape(TRIALS, 1, BLOCKS),
-        block_offset.reshape(TRIALS, BLOCKS),
-        flags,
-        shifts,
-        shifts,
-        past_steps,
-        past_changes,
-        jnp.asarray(inner_pair),
-        jnp.asarray(outer_pair),
-        jnp.asarray(twiddle),
-    )
+    )(*large, flags, shifts, shifts)
 
 
 def solution(mesh):

time: 63 us -> 55.2 us (0.88)
  Pallas kernels: 59.3 us -> 51.5 us
    pallas_call x1, Pallas kernels: 59.3 us -> 51.5 us  [local(): pl.pallas_call(step_kernel, out_shape=(jax.ShapeDtypeStruct((1, TRIALS),...]
where the time goes in v3:
time: 55.2 us; the launch traced here: 55 us
  Pallas kernels  51.5 us (93%)
  local copies, waits for them, and re-layouts  2.25 us (4%)
  between operations  1.29 us (2%)
    pallas_call x1, Pallas kernels, local(): pl.pallas_call(step_kernel, out_shape=(jax.ShapeDtypeStruct((1, TRIALS),...  51.5 us
    unnamed x2, local copies, waits for them, and re-layouts  2.25 us

profile of v3, /device:TPU:1, one launch (start us, length us, event | category | flops | bytes accessed | tf_op | source)
XLA Modules:
  0.0 55.0 jit_solution(1498398602208794430)
XLA Ops:
  1.3 51.5 %shard_map.140 = (f32[1,8]{1,0:T(1,128)}, f32[1,24]{1,0:T(1,128)}) custom-call(bf16[13824,128]{1,0:T(8,128)(2,1)} %bitcast.4, bf16[8,128,128]{2,1,0:T(8,128)(2,1)} %maps_hbm.1, bf16[1,32,32,32]{3,2,1,0:T(8,128)(2,1)} %volume_hbm.1, s32[256,128]{1,0:T(8,128)} %bitcast.5, s32[8,1,256]{2,1,0:T(1,128)} %bitcast.6, s32[8,256]{1,0:T(8,128)} %bitcast.7, ...), custom_call_target="tpu_custom_call" | custom-call | tf_op jit(solution)/shard_map/pallas_call | solution.py:682
  52.8 1.1 %copy.18 = f32[1,8]{1,0:T(1,128)} copy(f32[1,8]{1,0:T(1,128)} %get-tuple-element.4) | data formatting | bytes 64
  53.9 1.1 %copy.19 = f32[1,24]{1,0:T(1,128)} copy(f32[1,24]{1,0:T(1,128)} %get-tuple-element.5) | data formatting | bytes 192

commit v4 on v3

--- a/solution.py
+++ b/solution.py
@@ -19,8 +19,8 @@
 SLABS = 8
 NEAR = 6
 MESH = pl.DeviceIdType.MESH
-CHUNK = 768
-FIRST_CHUNKS = 3
+CHUNK = 1728
+FIRST_CHUNKS = 2
 F32 = jnp.float32
 BF16 = jnp.bfloat16
 
@@ -303,6 +303,87 @@
     )
     mapped[row_count : row_count + 8, :] += mapped[0:8, :]
 
+    for n in (5, 6, 7, 9, 10):
+        loads[n].wait()
+
+    turn_r, turn_i = twiddle_ref[0][None], twiddle_ref[1][None]
+
+    def spectrum(volume_rows):
+        first = dot(volume_rows, inner_ref[0]) + dot(volume_rows, inner_ref[1])
+        first = first.reshape(EDGE, 8, 2 * LANES)
+        first_r, first_i = first[:, :, :LANES], first[:, :, LANES:]
+        second = jnp.concatenate(
+            [first_r * turn_r - first_i * turn_i, first_r * turn_i + first_i * turn_r],
+            axis=-1,
+        ).reshape(BLOCKS, 2 * LANES)
+        second_high = second.astype(BF16)
+        second_low = (second - second_high.astype(F32)).astype(BF16)
+        third = (
+            dot(outer_ref[0], second_high)
+            + dot(outer_ref[0], second_low)
+            + dot(outer_ref[1], second_high)
+        )
+        return (
+            third[:BLOCKS, :LANES] - third[BLOCKS:, LANES:],
+            third[:BLOCKS, LANES:] + third[BLOCKS:, :LANES],
+        )
+
+    spec_r, spec_i = spectrum(info_out[:BLOCKS, :])
+    weight = wedge_ref[...].astype(F32)
+    weighted[0] = weight * spec_r
+    weighted[1] = weight * spec_i
+    weighted[2] = weight
+    power_particle = jnp.sum(
+        jnp.sum(weight * (spec_r * spec_r + spec_i * spec_i), axis=0, keepdims=True),
+        axis=1,
+        keepdims=True,
+    )
+
+    unit = 2.0 * math.pi / EDGE
+    freq_two = signed(4 * sub + lane // 32)
+    freq_three = signed(lane % 32)
+    freq_line = signed(lane)
+    shift_one = jnp.zeros((8, LANES), F32)
+    for t in range(TRIALS):
+        angle = unit * (
+            freq_two * shift_smem[0, 3 * t + 1] + freq_three * shift_smem[0, 3 * t + 2]
+        )
+        phase_tables[0, t] = jnp.cos(angle)
+        phase_tables[1, t] = jnp.sin(angle)
+        shift_one = jnp.where(sub == t, shift_smem[0, 3 * t], shift_one)
+    angle = unit * freq_line * shift_one
+    cos_line, sin_line = jnp.cos(angle), jnp.sin(angle)
+    line_tables[0] = cos_line
+    line_tables[1] = sin_line
+    line_tables[2] = freq_line * cos_line
+    line_tables[3] = freq_line * sin_line
+    line_copy = pltpu.make_async_copy(line_tables, line_smem, line_local)
+    line_copy.start()
+
+    place_rows = []
+    for t in range(TRIALS):
+        step = (slab_rows[t] // 2 - y_at + 4) % 4
+        near = jnp.where(step == 3, 2, step) * 2 + slab_rows[t] % 2
+        near = jnp.where(step == 2, -2 * SLABS, near - slab_rows[t])
+        place_rows.append(slots[t : t + 1] + (CAP * near).astype(F32))
+    slot_columns = 2.0 * jnp.transpose(jnp.concatenate(place_rows, axis=0))
+    hot_iota = lax.broadcasted_iota(jnp.int32, (BLOCKS, NEAR * LANES), 1).astype(F32)
+    for t in range(TRIALS):
+        column = slot_columns[:, t : t + 1]
+        hot[t, :BLOCKS, :] = jnp.where(hot_iota == column, 1.0, 0.0).astype(BF16)
+        hot[t, BLOCKS:, :] = jnp.where(hot_iota == column + 1.0, 1.0, 0.0).astype(BF16)
+
+    basis[...] = jnp.zeros((8, LANES), F32)
+    for i in range(HIST):
+        basis[i : i + 1, : 3 * TRIALS] = steps_ref[i]
+        basis[HIST + i : HIST + i + 1, : 3 * TRIALS] = changes_ref[i]
+    vectors = basis[...]
+    gram = jnp.zeros((8, LANES), F32)
+    for j in range(8):
+        gram = jnp.where(
+            lane == j, jnp.sum(vectors * vectors[j : j + 1], axis=1, keepdims=True), gram
+        )
+
     def to_smem(source, peer):
         return pltpu.make_async_copy(source, asked_smem.at[peer], ask_local.at[peer])
 
@@ -365,87 +446,6 @@
         return carry
 
     lax.fori_loop(0, 8, pick_far, 0)
-
-    for n in (5, 6, 7, 9, 10):
-        loads[n].wait()
-
-    turn_r, turn_i = twiddle_ref[0][None], twiddle_ref[1][None]
-
-    def spectrum(volume_rows):
-        first = dot(volume_rows, inner_ref[0]) + dot(volume_rows, inner_ref[1])
-        first = first.reshape(EDGE, 8, 2 * LANES)
-        first_r, first_i = first[:, :, :LANES], first[:, :, LANES:]
-        second = jnp.concatenate(
-            [first_r * turn_r - first_i * turn_i, first_r * turn_i + first_i * turn_r],
-            axis=-1,
-        ).reshape(BLOCKS, 2 * LANES)
-        second_high = second.astype(BF16)
-        second_low = (second - second_high.astype(F32)).astype(BF16)
-        third = (
-            dot(outer_ref[0], second_high)
-            + dot(outer_ref[0], second_low)
-            + dot(outer_ref[1], second_high)
-        )
-        return (
-            third[:BLOCKS, :LANES] - third[BLOCKS:, LANES:],
-            third[:BLOCKS, LANES:] + third[BLOCKS:, :LANES],
-        )
-
-    spec_r, spec_i = spectrum(info_out[:BLOCKS, :])
-    weight = wedge_ref[...].astype(F32)
-    weighted[0] = weight * spec_r
-    weighted[1] = weight * spec_i
-    weighted[2] = weight
-    power_particle = jnp.sum(
-        jnp.sum(weight * (spec_r * spec_r + spec_i * spec_i), axis=0, keepdims=True),
-        axis=1,
-        keepdims=True,
-    )
-
-    unit = 2.0 * math.pi / EDGE
-    freq_two = signed(4 * sub + lane // 32)
-    freq_three = signed(lane % 32)
-    freq_line = signed(lane)
-    shift_one = jnp.zeros((8, LANES), F32)
-    for t in range(TRIALS):
-        angle = unit * (
-            freq_two * shift_smem[0, 3 * t + 1] + freq_three * shift_smem[0, 3 * t + 2]
-        )
-        phase_tables[0, t] = jnp.cos(angle)
-        phase_tables[1, t] = jnp.sin(angle)
-        shift_one = jnp.where(sub == t, shift_smem[0, 3 * t], shift_one)
-    angle = unit * freq_line * shift_one
-    cos_line, sin_line = jnp.cos(angle), jnp.sin(angle)
-    line_tables[0] = cos_line
-    line_tables[1] = sin_line
-    line_tables[2] = freq_line * cos_line
-    line_tables[3] = freq_line * sin_line
-    line_copy = pltpu.make_async_copy(line_tables, line_smem, line_local)
-    line_copy.start()
-
-    place_rows = []
-    for t in range(TRIALS):
-        step = (slab_rows[t] // 2 - y_at + 4) % 4
-        near = jnp.where(step == 3, 2, step) * 2 + slab_rows[t] % 2
-        near = jnp.where(step == 2, -2 * SLABS, near - slab_rows[t])
-        place_rows.append(slots[t : t + 1] + (CAP * near).astype(F32))
-    slot_columns = 2.0 * jnp.transpose(jnp.concatenate(place_rows, axis=0))
-    hot_iota = lax.broadcasted_iota(jnp.int32, (BLOCKS, NEAR * LANES), 1).astype(F32)
-    for t in range(TRIALS):
-        column = slot_columns[:, t : t + 1]
-        hot[t, :BLOCKS, :] = jnp.where(hot_iota == column, 1.0, 0.0).astype(BF16)
-        hot[t, BLOCKS:, :] = jnp.where(hot_iota == column + 1.0, 1.0, 0.0).astype(BF16)
-
-    basis[...] = jnp.zeros((8, LANES), F32)
-    for i in range(HIST):
-        basis[i : i + 1, : 3 * TRIALS] = steps_ref[i]
-        basis[HIST + i : HIST + i + 1, : 3 * TRIALS] = changes_ref[i]
-    vectors = basis[...]
-    gram = jnp.zeros((8, LANES), F32)
-    for j in range(8):
-        gram = jnp.where(
-            lane == j, jnp.sum(vectors * vectors[j : j + 1], axis=1, keepdims=True), gram
-        )
 
     block_iota = lax.broadcasted_iota(jnp.int32, (LANES, BLOCKS), 1).astype(F32)
     slot_lane = lax.broadcasted_iota(jnp.int32, (LANES, LANES), 1)

time: 55.2 us -> 54 us (0.978)
  Pallas kernels: 51.5 us -> 50.3 us
    pallas_call x1, Pallas kernels: 51.5 us -> 50.3 us  [local(): pl.pallas_call(step_kernel, out_shape=(jax.ShapeDtypeStruct((1, TRIALS),...]
where the time goes in v4:
time: 54 us; the launch traced here: 53.8 us
  Pallas kernels  50.3 us (93%)
  local copies, waits for them, and re-layouts  2.25 us (4%)
  between operations  1.29 us (2%)
    pallas_call x1, Pallas kernels, local(): pl.pallas_call(step_kernel, out_shape=(jax.ShapeDtypeStruct((1, TRIALS),...  50.3 us
    unnamed x2, local copies, waits for them, and re-layouts  2.25 us

profile of v4, /device:TPU:1, one launch (start us, length us, event | category | flops | bytes accessed | tf_op | source)
XLA Modules:
  0.0 53.8 jit_solution(4475357795799126403)
XLA Ops:
  1.3 50.3 %shard_map.140 = (f32[1,8]{1,0:T(1,128)}, f32[1,24]{1,0:T(1,128)}) custom-call(bf16[13824,128]{1,0:T(8,128)(2,1)} %bitcast.4, bf16[8,128,128]{2,1,0:T(8,128)(2,1)} %maps_hbm.1, bf16[1,32,32,32]{3,2,1,0:T(8,128)(2,1)} %volume_hbm.1, s32[256,128]{1,0:T(8,128)} %bitcast.5, s32[8,1,256]{2,1,0:T(1,128)} %bitcast.6, s32[8,256]{1,0:T(8,128)} %bitcast.7, ...), custom_call_target="tpu_custom_call" | custom-call | tf_op jit(solution)/shard_map/pallas_call | solution.py:682
  51.6 1.1 %copy.18 = f32[1,8]{1,0:T(1,128)} copy(f32[1,8]{1,0:T(1,128)} %get-tuple-element.4) | data formatting | bytes 64
  52.7 1.1 %copy.19 = f32[1,24]{1,0:T(1,128)} copy(f32[1,24]{1,0:T(1,128)} %get-tuple-element.5) | data formatting | bytes 192

commit v5 on v4

--- a/solution.py
+++ b/solution.py
@@ -19,8 +19,8 @@
 SLABS = 8
 NEAR = 6
 MESH = pl.DeviceIdType.MESH
-CHUNK = 1728
-FIRST_CHUNKS = 2
+CHUNK = 3456
+FIRST_CHUNKS = 1
 F32 = jnp.float32
 BF16 = jnp.bfloat16
 
@@ -421,8 +421,8 @@
 
     def pick_trials(u, carry):
         def pick_peer(n, inner):
-            step = n + 1 + 3 * (n // 2) - (n // 4) * (8 - 2 * core)
-            peer = lax.rem(slab + step, 8)
+            step = 1 + 2 * lax.rem(n, 2) - n // 4
+            peer = lax.rem(y_at + step, 4) * 2 + n // 2 - (n // 4) * (1 + core)
             pick(peer, u, staged)
             sent[peer, u] = staged[...].astype(BF16)
             data(peer, u).start()

time: 54 us -> 53.7 us (level)
  no operation moved by 1% of the time
where the time goes in v5:
time: 53.7 us; the launch traced here: 53.5 us
  Pallas kernels  50 us (93%)
  local copies, waits for them, and re-layouts  2.25 us (4%)
  between operations  1.29 us (2%)
    pallas_call x1, Pallas kernels, local(): pl.pallas_call(step_kernel, out_shape=(jax.ShapeDtypeStruct((1, TRIALS),...  50 us
    unnamed x2, local copies, waits for them, and re-layouts  2.25 us

profile of v5, /device:TPU:1, one launch (start us, length us, event | category | flops | bytes accessed | tf_op | source)
XLA Modules:
  0.0 53.5 jit_solution(8807880697643684135)
XLA Ops:
  1.3 50.0 %shard_map.140 = (f32[1,8]{1,0:T(1,128)}, f32[1,24]{1,0:T(1,128)}) custom-call(bf16[13824,128]{1,0:T(8,128)(2,1)} %bitcast.4, bf16[8,128,128]{2,1,0:T(8,128)(2,1)} %maps_hbm.1, bf16[1,32,32,32]{3,2,1,0:T(8,128)(2,1)} %volume_hbm.1, s32[256,128]{1,0:T(8,128)} %bitcast.5, s32[8,1,256]{2,1,0:T(1,128)} %bitcast.6, s32[8,256]{1,0:T(8,128)} %bitcast.7, ...), custom_call_target="tpu_custom_call" | custom-call | tf_op jit(solution)/shard_map/pallas_call | solution.py:682
  51.3 1.1 %copy.18 = f32[1,8]{1,0:T(1,128)} copy(f32[1,8]{1,0:T(1,128)} %get-tuple-element.4) | data formatting | bytes 64
  52.4 1.1 %copy.19 = f32[1,24]{1,0:T(1,128)} copy(f32[1,24]{1,0:T(1,128)} %get-tuple-element.5) | data formatting | bytes 192
